TPU v7x, 256 devices: a whole 4x4x8 slice. The times are simulated.
256 devices in a mesh: frames: 8 (over x, y_hi), rows: 32 (over z, y_lo, core).
Axes of the slice: x: 4, y: 4 (y_hi: 2, y_lo: 2; y = y_hi * 2 + y_lo), z: 8, core: 2. Of those that a mesh axis runs over, the one named last changes fastest.
Arguments:
- series: bfloat16 [128, 1, 256, 256], P('frames', None, 'rows'), may hold values from -6 to 6
- lift_weight: bfloat16 [3, 3, 2, 64], replicated, may hold values from -1.5 to 1.5
- lift_bias: float32 [64], replicated, may hold values from -3 to 3
- mix_weight: bfloat16 [3, 3, 64, 64], replicated, may hold values from -0.25 to 0.25
- mix_bias: float32 [64], replicated, may hold values from -3 to 3
- proj_weight: bfloat16 [64, 2], replicated, may hold values from -0.75 to 0.75
- proj_bias: float32 [2], replicated, may hold values from -3 to 3
Outputs:
- refined: float32 [128, 1, 256, 256], P('frames', None, 'rows')
All inputs are finite; a program needn't handle non-finite values.
Results may differ from a plain program's by a relative error of at most 0.007.
Values may be sent and summed in bfloat16 or wider, within the bound.
A program may use at most 192 MiB of HBM per device.

v0:
```python
import math

import jax
import jax.numpy as jnp
from jax import lax
from jax.sharding import PartitionSpec as P


def padded_2(cells, sides, width):
    for axis, dim in sides:
        count = lax.axis_size(axis)
        ends = count - 1
        head = lax.slice_in_dim(cells, 0, width, axis=dim)
        tail = lax.slice_in_dim(cells, cells.shape[dim] - width, cells.shape[dim], axis=dim)
        cells = jnp.concatenate(
            [
                lax.ppermute(tail, axis, [(i, (i + 1) % count) for i in range(ends)]),
                cells,
                lax.ppermute(head, axis, [((i + 1) % count, i) for i in range(ends)]),
            ],
            axis=dim,
        )
    return cells


def phases(freq_idx, time_idx, total):
    wrapped = jnp.remainder((freq_idx[:, None] - total // 2) * time_idx[None, :], total)
    return 2.0 * math.pi / total * wrapped.astype(jnp.float32)


def fwd_table(freq_idx, time_idx, total):
    angles = phases(freq_idx, time_idx, total)
    factor = 1.0 / math.sqrt(total)
    return jnp.concatenate([jnp.cos(angles) * factor, -jnp.sin(angles) * factor], 0).astype(
        jnp.bfloat16
    )


def inv_table(time_idx, freq_idx, total):
    angles = phases(freq_idx, time_idx, total).T
    factor = 1.0 / math.sqrt(total)
    return jnp.concatenate([jnp.cos(angles) * factor, jnp.sin(angles) * factor], 0).astype(
        jnp.bfloat16
    )


def apply_table(table, values):
    height = table.shape[0] // 2
    flattened = values.reshape(values.shape[0], -1)
    product = jnp.dot(table, flattened, preferred_element_type=jnp.float32)
    product = product.reshape((2, height) + values.shape[1:])
    half_cols = values.shape[-1] // 2
    lower_part = product[1]
    return product[0] + jnp.concatenate(
        [-lower_part[..., half_cols:], lower_part[..., :half_cols]], -1
    )


def conv_first(region, lift_weight, lift_bias):
    n_freq = region.shape[0] - 2
    n_rows = region.shape[1] - 2
    half_cols = region.shape[2] // 2
    split_in = region.reshape(n_freq + 2, n_rows + 2, 2, half_cols)
    running = jnp.zeros((n_freq, n_rows, lift_weight.shape[3], half_cols), jnp.float32)
    for tap_row in range(3):
        for tap_col in range(3):
            running = running + jnp.einsum(
                "io,kric->kroc",
                lift_weight[tap_row, tap_col],
                split_in[tap_row : tap_row + n_freq, tap_col : tap_col + n_rows],
                preferred_element_type=jnp.float32,
            )
    hidden = jax.nn.relu(running + lift_bias[None, None, :, None])
    return hidden.astype(jnp.bfloat16)


def conv_rest(padded, mix_weight, mix_bias, proj_weight, proj_bias):
    n_freq = padded.shape[0] - 2
    n_rows = padded.shape[1] - 2
    running = jnp.zeros((n_freq, n_rows, mix_weight.shape[3], padded.shape[3]), jnp.float32)
    for tap_row in range(3):
        for tap_col in range(3):
            running = running + jnp.einsum(
                "io,kric->kroc",
                mix_weight[tap_row, tap_col],
                padded[tap_row : tap_row + n_freq, tap_col : tap_col + n_rows],
                preferred_element_type=jnp.float32,
            )
    mixed = jax.nn.relu(running + mix_bias[None, None, :, None]).astype(jnp.bfloat16)
    update = (
        jnp.einsum("io,kric->kroc", proj_weight, mixed, preferred_element_type=jnp.float32)
        + proj_bias[None, None, :, None]
    )
    return update.reshape(n_freq, n_rows, 2 * padded.shape[3]).astype(jnp.bfloat16)


def per_device(series, lift_weight, lift_bias, mix_weight, mix_bias, proj_weight, proj_bias):
    frame_count = series.shape[0]
    nframe = frame_count * lax.axis_size("frames")
    own_first = lax.axis_index("frames") * frame_count
    own_idx = own_first + jnp.arange(frame_count, dtype=jnp.int32)
    portion = lax.all_gather(series, "frames", axis=0, tiled=True)
    time_idx = jnp.arange(portion.shape[0], dtype=jnp.int32)
    spectrum = apply_table(fwd_table(own_idx, time_idx, nframe), portion).astype(jnp.bfloat16)
    bordered = padded_2(spectrum, (("frames", 0), ("rows", 2)), 1)
    hidden = conv_first(bordered[:, 0], lift_weight, lift_bias)
    padded = padded_2(hidden, (("frames", 0), ("rows", 1)), 1)
    updates = [conv_rest(padded, mix_weight, mix_bias, proj_weight, proj_bias)]
    update = jnp.stack(updates, 1)
    portion = lax.all_gather(update, "frames", axis=0, tiled=True)
    freq_idx = jnp.arange(portion.shape[0], dtype=jnp.int32)
    back = apply_table(inv_table(own_idx, freq_idx, nframe), portion)
    return series.astype(jnp.float32) + back


def solution(mesh):
    return jax.shard_map(
        per_device,
        mesh=mesh,
        in_specs=(P("frames", None, "rows", None), P(), P(), P(), P(), P(), P()),
        out_specs=P("frames", None, "rows", None),
        check_vma=False,
    )
```

profile of v0, /device:TPU:128, one launch (start us, length us, event | category | flops | bytes accessed | tf_op | source)
XLA Modules:
  0.0 171.4 jit_solution(7694256585223922557)
XLA Ops:
  0.1 35.1 %all_gather.6 = bf16[128,1,8,256]{3,2,1,0:T(8,128)(2,1)S(1)} all-gather(bf16[16,1,8,256]{3,2,1,0:T(8,128)(2,1)} %param.7), channel_id=1, replica_groups=mesh['frames'=8,'rows'=32] {'frames'}, dimensions={0}, use_global_device_ids=true | all-gather | bytes 589824 | tf_op jit(solution)/shard_map/all_gather | solution.py:102
  35.9 5.4 %collective-permute-start = (bf16[1,1,8,256]{3,0,2,1:T(2,128)(2,1)S(1)}, bf16[1,1,8,256]{3,0,2,1:T(2,128)(2,1)S(1)}, u32[]{:S(2)}, u32[]{:S(2)}) collective-permute-start(bf16[1,1,8,256]{3,0,2,1:T(2,128)(2,1)S(1)} %get-tuple-element.30), channel_id=1, source_target_pairs={{0,32},{32,64},{64,96},{96,128},{128,160},{160,192},{192,224},{1,3... | collective-permute-start | bytes 12296 | tf_op jit(solution)/shard_map/ppermute | solution.py:17
  41.3 1.3 collective-permute-start.1
  42.6 5.7 %collective-permute-done.1 = bf16[1,1,8,256]{3,0,2,1:T(2,128)(2,1)S(1)} collective-permute-done((bf16[1,1,8,256]{3,0,2,1:T(2,128)(2,1)S(1)}, bf16[1,1,8,256]{3,0,2,1:T(2,128)(2,1)S(1)}, u32[]{:S(2)}, u32[]{:S(2)}) %collective-permute-start.1) | collective-permute-done | bytes 4128 | tf_op jit(solution)/shard_map/ppermute | solution.py:19
  48.3 1.9 %collective-permute-start.2 = (bf16[18,1,1,256]{3,0,2,1:T(8,128)(2,1)S(1)}, bf16[18,1,1,256]{3,0,2,1:T(8,128)(2,1)S(1)}, u32[]{:S(2)}, u32[]{:S(2)}) collective-permute-start(bf16[18,1,1,256]{3,0,2,1:T(8,128)(2,1)S(1)} %get-tuple-element.28), channel_id=1, source_target_pairs={{0,1},{1,2},{2,3},{3,4},{4,5},{5,6},{6,7},{7,8},{8,9},{9,10},{10,1... | collective-permute-start | bytes 27656 | tf_op jit(solution)/shard_map/ppermute | solution.py:17
  50.3 5.8 %collective-permute-start.3 = (bf16[18,1,1,256]{3,0,2,1:T(8,128)(2,1)S(1)}, bf16[18,1,1,256]{3,0,2,1:T(8,128)(2,1)S(1)}, u32[]{:S(2)}, u32[]{:S(2)}) collective-permute-start(bf16[18,1,1,256]{3,0,2,1:T(8,128)(2,1)S(1)} %get-tuple-element.29), channel_id=1, source_target_pairs={{1,0},{2,1},{3,2},{4,3},{5,4},{6,5},{7,6},{8,7},{9,8},{10,9},{11,1... | collective-permute-start | bytes 27656 | tf_op jit(solution)/shard_map/ppermute | solution.py:19
  56.2 1.2 collective-permute-done.3
  57.8 0.7 fusion.43
  58.6 0.7 fusion.45
  59.3 0.7 fusion.47
  60.1 2.7 %fusion.49 = f32[16,8,128,64]{2,3,1,0:T(8,128)} fusion(bf16[16,8,2,128]{3,2,0,1:T(2,128)(2,1)S(1)} %get-tuple-element.23, bf16[3,3,2,64]{3,2,1,0:T(2,128)(2,1)S(1)} %copy-done.3), kind=kOutput, calls=%fused_computation.44 | convolution fusion | flops 4194304 | bytes 4260352 | tf_op jit(solution)/shard_map/io,kric->kroc/dot_general | solution.py:67
  62.8 2.8 %fusion.51 = f32[16,8,128,64]{2,3,1,0:T(8,128)} fusion(bf16[16,8,2,128]{3,2,0,1:T(2,128)(2,1)S(1)} %get-tuple-element.24, bf16[3,3,2,64]{3,2,1,0:T(2,128)(2,1)S(1)} %copy-done.3), kind=kOutput, calls=%fused_computation.46 | convolution fusion | flops 4194304 | bytes 4260352 | tf_op jit(solution)/shard_map/io,kric->kroc/dot_general | solution.py:67
  65.5 2.7 %fusion.53 = f32[16,8,128,64]{2,3,1,0:T(8,128)} fusion(bf16[16,8,2,128]{3,2,0,1:T(2,128)(2,1)S(1)} %get-tuple-element.25, bf16[3,3,2,64]{3,2,1,0:T(2,128)(2,1)S(1)} %copy-done.3), kind=kOutput, calls=%fused_computation.48 | convolution fusion | flops 4194304 | bytes 4260352 | tf_op jit(solution)/shard_map/io,kric->kroc/dot_general | solution.py:67
  68.3 2.7 %fusion.55 = f32[16,8,128,64]{2,3,1,0:T(8,128)} fusion(bf16[16,8,2,128]{3,2,0,1:T(2,128)(2,1)S(1)} %get-tuple-element.26, bf16[3,3,2,64]{3,2,1,0:T(2,128)(2,1)S(1)} %copy-done.3), kind=kOutput, calls=%fused_computation.50 | convolution fusion | flops 4194304 | bytes 4260352 | tf_op jit(solution)/shard_map/io,kric->kroc/dot_general | solution.py:67
  71.0 2.7 %fusion.57 = f32[16,8,128,64]{2,3,1,0:T(8,128)} fusion(bf16[16,8,2,128]{3,2,0,1:T(2,128)(2,1)S(1)} %get-tuple-element.27, bf16[3,3,2,64]{3,2,1,0:T(2,128)(2,1)S(1)} %copy-done.3), kind=kOutput, calls=%fused_computation.52 | convolution fusion | flops 4194304 | bytes 4260352 | tf_op jit(solution)/shard_map/io,kric->kroc/dot_general | solution.py:67
  73.7 8.7 %fusion.20 = bf16[16,8,64,128]{3,2,1,0:T(8,128)(2,1)S(1)} fusion(f32[64]{0:T(128)S(1)} %copy-done.4, f32[16,8,128,64]{2,3,1,0:T(8,128)S(1)} %fusion.43, f32[16,8,128,64]{2,3,1,0:T(8,128)S(1)} %fusion.45, f32[16,8,128,64]{2,3,1,0:T(8,128)S(1)} %fusion.47, f32[16,8,128,64]{2,3,1,0:T(8,128)} %fusion.49, f32[16,8,128,64]{2,3,1,0:T(8,128)} %fusion.51, ...), kind=kOutput, calls=%fused_computation.24 | convolution fusion | flops 15728640 | bytes 35718144 | tf_op jit(solution)/shard_map/io,kric->kroc/dot_general | solution.py:67
  82.4 2.8 %collective-permute-start.4 = (bf16[1,8,64,128]{3,2,1,0:T(8,128)(2,1)S(1)}, bf16[1,8,64,128]{3,2,1,0:T(8,128)(2,1)S(1)}, u32[]{:S(2)}, u32[]{:S(2)}) collective-permute-start(bf16[1,8,64,128]{3,2,1,0:T(8,128)(2,1)S(1)} %get-tuple-element.9), channel_id=1, source_target_pairs={{0,32},{32,64},{64,96},{96,128},{128,160},{160,192},{192,224},{1,3... | collective-permute-start | bytes 393224 | tf_op jit(solution)/shard_map/ppermute | solution.py:17
  85.3 1.3 collective-permute-start.5
  86.6 2.7 %fusion.64 = f32[16,8,128,64]{2,3,1,0:T(8,128)} fusion(bf16[16,8,64,128]{3,2,1,0:T(8,128)(2,1)S(1)} %fusion.20, bf16[3,3,64,64]{3,2,1,0:T(8,128)(2,1)S(1)} %copy-done.2), kind=kOutput, calls=%fused_computation.59 | convolution fusion | flops 134217728 | bytes 6307840 | tf_op jit(solution)/shard_map/io,kric->kroc/dot_general | solution.py:83
  89.2 4.4 %collective-permute-done.5 = bf16[1,8,64,128]{3,2,1,0:T(8,128)(2,1)S(1)} collective-permute-done((bf16[1,8,64,128]{3,2,1,0:T(8,128)(2,1)S(1)}, bf16[1,8,64,128]{3,2,1,0:T(8,128)(2,1)S(1)}, u32[]{:S(2)}, u32[]{:S(2)}) %collective-permute-start.5) | collective-permute-done | bytes 131104 | tf_op jit(solution)/shard_map/ppermute | solution.py:19
  93.7 1.9 %collective-permute-start.6 = (bf16[18,1,64,128]{3,2,1,0:T(8,128)(2,1)S(1)}, bf16[18,1,64,128]{3,2,1,0:T(8,128)(2,1)S(1)}, u32[]{:S(2)}, u32[]{:S(2)}) collective-permute-start(bf16[18,1,64,128]{3,2,1,0:T(8,128)(2,1)S(1)} %get-tuple-element.7), channel_id=1, source_target_pairs={{0,1},{1,2},{2,3},{3,4},{4,5},{5,6},{6,7},{7,8},{8,9},{9,10},{10,1... | collective-permute-start | bytes 884744 | tf_op jit(solution)/shard_map/ppermute | solution.py:17
  95.6 5.9 %collective-permute-start.7 = (bf16[18,1,64,128]{3,2,1,0:T(8,128)(2,1)S(1)}, bf16[18,1,64,128]{3,2,1,0:T(8,128)(2,1)S(1)}, u32[]{:S(2)}, u32[]{:S(2)}) collective-permute-start(bf16[18,1,64,128]{3,2,1,0:T(8,128)(2,1)S(1)} %get-tuple-element.8), channel_id=1, source_target_pairs={{1,0},{2,1},{3,2},{4,3},{5,4},{6,5},{7,6},{8,7},{9,8},{10,9},{11,1... | collective-permute-start | bytes 884744 | tf_op jit(solution)/shard_map/ppermute | solution.py:19
  101.6 2.7 %fusion.4 = f32[16,8,128,64]{2,3,1,0:T(8,128)} fusion(bf16[1,8,64,128]{3,2,1,0:T(8,128)(2,1)S(1)} %collective-permute-done.5, bf16[16,8,64,128]{3,2,1,0:T(8,128)(2,1)S(1)} %fusion.20, bf16[3,3,64,64]{3,2,1,0:T(8,128)(2,1)S(1)} %copy-done.2), kind=kOutput, calls=%fused_computation.7 | convolution fusion | flops 138412032 | bytes 6438912 | tf_op jit(solution)/shard_map/io,kric->kroc/dot_general | solution.py:83
  104.2 2.7 %fusion.14 = f32[16,8,128,64]{2,3,1,0:T(8,128)} fusion(bf16[16,8,64,128]{3,2,1,0:T(8,128)(2,1)S(1)} %fusion.20, bf16[1,8,64,128]{3,2,1,0:T(8,128)(2,1)S(1)} %collective-permute-done.4, bf16[3,3,64,64]{3,2,1,0:T(8,128)(2,1)S(1)} %copy-done.2), kind=kOutput, calls=%fused_computation.18 | convolution fusion | flops 138412032 | bytes 6438912 | tf_op jit(solution)/shard_map/io,kric->kroc/dot_general | solution.py:83
  106.9 0.8 maximum_maximum_fusion
  107.8 2.7 %fusion.6 = f32[16,8,128,64]{2,3,1,0:T(8,128)} fusion(bf16[18,9,64,128]{3,2,1,0:T(8,128)(2,1)S(1)} %get-tuple-element.5, bf16[3,3,64,64]{3,2,1,0:T(8,128)(2,1)S(1)} %copy-done.2), kind=kOutput, calls=%fused_computation.9 | convolution fusion | flops 134217728 | bytes 6307840 | tf_op jit(solution)/shard_map/io,kric->kroc/dot_general | solution.py:83
  110.5 2.7 %fusion.10 = f32[16,8,128,64]{2,3,1,0:T(8,128)} fusion(bf16[18,9,64,128]{3,2,1,0:T(8,128)(2,1)S(1)} %get-tuple-element.5, bf16[3,3,64,64]{3,2,1,0:T(8,128)(2,1)S(1)} %copy-done.2), kind=kOutput, calls=%fused_computation.13 | convolution fusion | flops 134217728 | bytes 6307840 | tf_op jit(solution)/shard_map/io,kric->kroc/dot_general | solution.py:83
  113.2 2.7 %fusion.16 = f32[16,8,128,64]{2,3,1,0:T(8,128)} fusion(bf16[18,9,64,128]{3,2,1,0:T(8,128)(2,1)S(1)} %get-tuple-element.5, bf16[3,3,64,64]{3,2,1,0:T(8,128)(2,1)S(1)} %copy-done.2), kind=kOutput, calls=%fused_computation.20 | convolution fusion | flops 134217728 | bytes 6307840 | tf_op jit(solution)/shard_map/io,kric->kroc/dot_general | solution.py:83
  115.9 2.7 %fusion.8 = f32[16,8,128,64]{2,3,1,0:T(8,128)} fusion(bf16[18,9,64,128]{3,2,1,0:T(8,128)(2,1)S(1)} %get-tuple-element.6, bf16[3,3,64,64]{3,2,1,0:T(8,128)(2,1)S(1)} %copy-done.2), kind=kOutput, calls=%fused_computation.11 | convolution fusion | flops 134217728 | bytes 6307840 | tf_op jit(solution)/shard_map/io,kric->kroc/dot_general | solution.py:83
  118.6 2.8 %fusion.12 = f32[16,8,128,64]{2,3,1,0:T(8,128)} fusion(bf16[18,9,64,128]{3,2,1,0:T(8,128)(2,1)S(1)} %get-tuple-element.6, bf16[3,3,64,64]{3,2,1,0:T(8,128)(2,1)S(1)} %copy-done.2), kind=kOutput, calls=%fused_computation.15 | convolution fusion | flops 134217728 | bytes 6307840 | tf_op jit(solution)/shard_map/io,kric->kroc/dot_general | solution.py:83
  121.4 13.4 %fusion.35 = bf16[16,8,2,128]{3,2,1,0:T(2,128)(2,1)S(1)} fusion(f32[64]{0:T(128)S(1)} %copy-done.5, bf16[18,9,64,128]{3,2,1,0:T(8,128)(2,1)S(1)} %get-tuple-element.6, f32[16,8,128,64]{2,3,1,0:T(8,128)} %fusion.4, f32[16,8,128,64]{2,3,1,0:T(8,128)} %fusion.6, f32[16,8,128,64]{2,3,1,0:T(8,128)} %fusion.8, f32[16,8,128,64]{2,3,1,0:T(8,128)} %fusion.64, ...), kind=kOutput, calls=%fused_computation.27 | convolution fusion | flops 150011904 | bytes 35735040 | tf_op jit(solution)/shard_map/io,kric->kroc/dot_general | solution.py:91
  134.9 35.4 %all_gather.7 = bf16[128,1,8,256]{3,2,1,0:T(8,128)(2,1)S(1)} all-gather(bf16[16,1,8,256]{3,2,1,0:T(8,128)(2,1)S(1)} %bitcast.199), channel_id=1, replica_groups=mesh['frames'=8,'rows'=32] {'frames'}, dimensions={0}, use_global_device_ids=true | all-gather | bytes 589824 | tf_op jit(solution)/shard_map/all_gather | solution.py:110
  (47 shorter events, 2.5 us)
Async XLA Ops:
  0.0 121.4 %copy-start = (bf16[64,2]{0,1:T(2,128)(2,1)S(1)}, bf16[64,2]{0,1:T(2,128)(2,1)}, u32[]{:S(2)}) copy-start(bf16[64,2]{0,1:T(2,128)(2,1)} %param.12) | copy-start | bytes 772
  0.0 57.8 %copy-start.3 = (bf16[3,3,2,64]{3,2,1,0:T(2,128)(2,1)S(1)}, bf16[3,3,2,64]{3,2,1,0:T(2,128)(2,1)}, u32[]{:S(2)}) copy-start(bf16[3,3,2,64]{3,2,1,0:T(2,128)(2,1)} %param.8) | copy-start | bytes 6916
  35.9 6.7 %collective-permute-start = (bf16[1,1,8,256]{3,0,2,1:T(2,128)(2,1)S(1)}, bf16[1,1,8,256]{3,0,2,1:T(2,128)(2,1)S(1)}, u32[]{:S(2)}, u32[]{:S(2)}) collective-permute-start(bf16[1,1,8,256]{3,0,2,1:T(2,128)(2,1)S(1)} %get-tuple-element.30), channel_id=1, source_target_pairs={{0,32},{32,64},{64,96},{96,128},{128,160},{160,192},{192,224},{1,3... | collective-permute-start | bytes 12296 | tf_op jit(solution)/shard_map/ppermute | solution.py:17
  41.3 7.0 %collective-permute-start.1 = (bf16[1,1,8,256]{3,0,2,1:T(2,128)(2,1)S(1)}, bf16[1,1,8,256]{3,0,2,1:T(2,128)(2,1)S(1)}, u32[]{:S(2)}, u32[]{:S(2)}) collective-permute-start(bf16[1,1,8,256]{3,0,2,1:T(2,128)(2,1)S(1)} %get-tuple-element.31), channel_id=1, source_target_pairs={{32,0},{64,32},{96,64},{128,96},{160,128},{192,160},{224,192},{33,... | collective-permute-start | bytes 12296 | tf_op jit(solution)/shard_map/ppermute | solution.py:19
  48.3 7.8 %collective-permute-start.2 = (bf16[18,1,1,256]{3,0,2,1:T(8,128)(2,1)S(1)}, bf16[18,1,1,256]{3,0,2,1:T(8,128)(2,1)S(1)}, u32[]{:S(2)}, u32[]{:S(2)}) collective-permute-start(bf16[18,1,1,256]{3,0,2,1:T(8,128)(2,1)S(1)} %get-tuple-element.28), channel_id=1, source_target_pairs={{0,1},{1,2},{2,3},{3,4},{4,5},{5,6},{6,7},{7,8},{8,9},{9,10},{10,1... | collective-permute-start | bytes 27656 | tf_op jit(solution)/shard_map/ppermute | solution.py:17
  50.3 7.1 %collective-permute-start.3 = (bf16[18,1,1,256]{3,0,2,1:T(8,128)(2,1)S(1)}, bf16[18,1,1,256]{3,0,2,1:T(8,128)(2,1)S(1)}, u32[]{:S(2)}, u32[]{:S(2)}) collective-permute-start(bf16[18,1,1,256]{3,0,2,1:T(8,128)(2,1)S(1)} %get-tuple-element.29), channel_id=1, source_target_pairs={{1,0},{2,1},{3,2},{4,3},{5,4},{6,5},{7,6},{8,7},{9,8},{10,9},{11,1... | collective-permute-start | bytes 27656 | tf_op jit(solution)/shard_map/ppermute | solution.py:19
  68.3 5.4 %copy-start.4 = (f32[64]{0:T(128)S(1)}, f32[64]{0:T(128)}, u32[]{:S(2)}) copy-start(f32[64]{0:T(128)} %param.9) | copy-start | bytes 772
  73.7 12.9 %copy-start.2 = (bf16[3,3,64,64]{3,2,1,0:T(8,128)(2,1)S(1)}, bf16[3,3,64,64]{3,2,1,0:T(8,128)(2,1)}, u32[]{:S(2)}) copy-start(bf16[3,3,64,64]{3,2,1,0:T(8,128)(2,1)} %param.10) | copy-start | bytes 221188
  82.4 6.8 %collective-permute-start.4 = (bf16[1,8,64,128]{3,2,1,0:T(8,128)(2,1)S(1)}, bf16[1,8,64,128]{3,2,1,0:T(8,128)(2,1)S(1)}, u32[]{:S(2)}, u32[]{:S(2)}) collective-permute-start(bf16[1,8,64,128]{3,2,1,0:T(8,128)(2,1)S(1)} %get-tuple-element.9), channel_id=1, source_target_pairs={{0,32},{32,64},{64,96},{96,128},{128,160},{160,192},{192,224},{1,3... | collective-permute-start | bytes 393224 | tf_op jit(solution)/shard_map/ppermute | solution.py:17
  85.3 8.4 %collective-permute-start.5 = (bf16[1,8,64,128]{3,2,1,0:T(8,128)(2,1)S(1)}, bf16[1,8,64,128]{3,2,1,0:T(8,128)(2,1)S(1)}, u32[]{:S(2)}, u32[]{:S(2)}) collective-permute-start(bf16[1,8,64,128]{3,2,1,0:T(8,128)(2,1)S(1)} %get-tuple-element.10), channel_id=1, source_target_pairs={{32,0},{64,32},{96,64},{128,96},{160,128},{192,160},{224,192},{33,... | collective-permute-start | bytes 393224 | tf_op jit(solution)/shard_map/ppermute | solution.py:19
  93.7 13.2 %collective-permute-start.6 = (bf16[18,1,64,128]{3,2,1,0:T(8,128)(2,1)S(1)}, bf16[18,1,64,128]{3,2,1,0:T(8,128)(2,1)S(1)}, u32[]{:S(2)}, u32[]{:S(2)}) collective-permute-start(bf16[18,1,64,128]{3,2,1,0:T(8,128)(2,1)S(1)} %get-tuple-element.7), channel_id=1, source_target_pairs={{0,1},{1,2},{2,3},{3,4},{4,5},{5,6},{6,7},{7,8},{8,9},{9,10},{10,1... | collective-permute-start | bytes 884744 | tf_op jit(solution)/shard_map/ppermute | solution.py:17
  95.6 11.3 %collective-permute-start.7 = (bf16[18,1,64,128]{3,2,1,0:T(8,128)(2,1)S(1)}, bf16[18,1,64,128]{3,2,1,0:T(8,128)(2,1)S(1)}, u32[]{:S(2)}, u32[]{:S(2)}) collective-permute-start(bf16[18,1,64,128]{3,2,1,0:T(8,128)(2,1)S(1)} %get-tuple-element.8), channel_id=1, source_target_pairs={{1,0},{2,1},{3,2},{4,3},{5,4},{6,5},{7,6},{8,7},{9,8},{10,9},{11,1... | collective-permute-start | bytes 884744 | tf_op jit(solution)/shard_map/ppermute | solution.py:19
  118.6 2.8 %copy-start.5 = (f32[64]{0:T(128)S(1)}, f32[64]{0:T(128)}, u32[]{:S(2)}) copy-start(f32[64]{0:T(128)} %param.11) | copy-start | bytes 772
  118.6 2.8 %copy-start.6 = (f32[2]{0:T(128)S(1)}, f32[2]{0:T(128)}, u32[]{:S(2)}) copy-start(f32[2]{0:T(128)} %param.13) | copy-start | bytes 28
  121.4 49.3 %copy-start.1 = (bf16[16,1,8,256]{3,2,1,0:T(8,128)(2,1)S(1)}, bf16[16,1,8,256]{3,2,1,0:T(8,128)(2,1)}, u32[]{:S(2)}) copy-start(bf16[16,1,8,256]{3,2,1,0:T(8,128)(2,1)} %param.7) | copy-start | bytes 196612
where the time goes:
time: 172 us; the launch traced here: 171 us
  blocking collectives  70.5 us (41%)
  matrix products  60 us (35%)
  starting transfers between devices  26.3 us (15%)
  waiting for transfers between devices  11.4 us (7%)
  other arithmetic  2 us (1%)
    all_gather x1, blocking collectives, per_device(): portion = lax.all_gather(update, 'frames', axis=0, tiled=True)  35.4 us
    all_gather x1, blocking collectives, per_device(): portion = lax.all_gather(series, 'frames', axis=0, tiled=True)  35.1 us
    dot_general x9, matrix products, conv_first(): jnp.einsum('io,kric->kroc', lift_weight[tap_row, tap_col], split_in[tap_r...  24.5 us
    dot_general x8, matrix products, conv_rest(): jnp.einsum('io,kric->kroc', mix_weight[tap_row, tap_col], padded[tap_row:...  21.6 us
    ppermute x4, starting transfers between devices, padded_2(): lax.ppermute(head, axis, [((i + 1) % count, i) for i in range(ends)])  14.3 us
    dot_general x1, matrix products, conv_rest(): jnp.einsum('io,kric->kroc', proj_weight, mixed, preferred_element_type=jn...  13.4 us
    ppermute x4, starting transfers between devices, padded_2(): lax.ppermute(tail, axis, [(i, (i + 1) % count) for i in range(ends)])  12.1 us
    ppermute x4, waiting for transfers between devices, padded_2(): lax.ppermute(head, axis, [((i + 1) % count, i) for i in range(ends)])  11.3 us
  transfers between devices with their start and end apart: 8, of which 3 were waited for; matrix products, arithmetic and copies ran while one was open for 5% of the time, Pallas kernels for 0%

commit v1 on v0

v1 whole, which is shorter than its diff:
```python
import functools
import math

import jax
import jax.numpy as jnp
import ml_dtypes
import numpy as np
from jax import lax
from jax.experimental import pallas as pl
from jax.experimental.pallas import tpu as pltpu
from jax.sharding import PartitionSpec as P

MESH = pl.DeviceIdType.MESH
BF16 = jnp.bfloat16
F32 = jnp.float32

NF = 8
T = 16
N = 128
R = 8
C = 16
O = 64
KB = 4
NB = N // KB
G = 16
NG = N // G
W = G + 2


def forward_table():
    k = np.arange(N)
    t = np.arange(N)
    angle = (2.0 * math.pi / N * (((k[:, None] - N // 2) * t[None, :]) % N)).astype(np.float32)
    scale = np.float32(1.0 / math.sqrt(N))
    re = (np.cos(angle) * scale).astype(ml_dtypes.bfloat16).astype(np.float32)
    im = (-np.sin(angle) * scale).astype(ml_dtypes.bfloat16).astype(np.float32)
    full = np.zeros((NF, 2, T, NG, 128), np.float32)
    for g in range(NG):
        for w in range(W):
            kk = g * G + w - 1
            if not 0 <= kk < N:
                continue
            a = re[kk].reshape(NF, T)
            b = im[kk].reshape(NF, T)
            for tap in range(3):
                lane = tap * 2 * W + w * 2
                full[:, 0, :, g, lane] = a
                full[:, 1, :, g, lane] = -b
                full[:, 0, :, g, lane + 1] = b
                full[:, 1, :, g, lane + 1] = a
    return full.reshape(NF * 2 * T, NG * 128).astype(ml_dtypes.bfloat16)


def inverse_table():
    k = np.arange(N)
    t = np.arange(N)
    angle = (2.0 * math.pi / N * (((k[:, None] - N // 2) * t[None, :]) % N)).astype(np.float32).T
    scale = np.float32(1.0 / math.sqrt(N))
    re = (np.cos(angle) * scale).reshape(NF, T, N)
    im = (np.sin(angle) * scale).reshape(NF, T, N)
    full = np.zeros((NF, 2, T, N, 2), np.float32)
    full[:, 0, :, :, 0] = re
    full[:, 0, :, :, 1] = -im
    full[:, 1, :, :, 0] = im
    full[:, 1, :, :, 1] = re
    return full.reshape(NF * 2 * T, N * 2).astype(ml_dtypes.bfloat16)


def place_table():
    full = np.zeros((G // KB, 128, KB, 32), np.float32)
    for q in range(G // KB):
        for j in range(KB):
            for a in range(3):
                for b in range(3):
                    for i in range(2):
                        full[q, b * 2 * W + (q * KB + j + a) * 2 + i, j, (a * 3 + b) * 2 + i] = 1
    return full.reshape(G // KB, 128, 128).astype(ml_dtypes.bfloat16)


def butterfly(parts):
    lane = lax.broadcasted_iota(jnp.int32, parts[0].shape, 1)
    for bit in range(3):
        step = 1 << bit
        upper = ((lane >> (4 + bit)) & 1) == 1
        out = list(parts)
        for i in range(8):
            if i & step:
                continue
            lo, hi = parts[i], parts[i + step]
            out[i] = jnp.where(upper, pltpu.roll(hi, 16 * step, 1), lo)
            out[i + step] = jnp.where(upper, hi, pltpu.roll(lo, 128 - 16 * step, 1))
        parts = out
    return parts


def kernel(
    n_rows,
    series,
    fwd,
    inv,
    place,
    lift4,
    lift_bias,
    mix,
    mix_bias,
    proj,
    proj_bias,
    out,
    series_v,
    fwd_v,
    inv_v,
    place_v,
    lift4_v,
    lift_bias_v,
    mix_v,
    mix_bias_v,
    proj_v,
    proj_bias_v,
    series_f,
    sent,
    got,
    xt,
    halo,
    spec,
    patch_a,
    patch_b,
    lift_m,
    mix_m,
    hid,
    upd,
    sent2,
    got2,
    load_sem,
    send_sem,
    recv_sem,
    halo_send_sem,
    halo_recv_sem,
    send2_sem,
    recv2_sem,
):
    f = lax.axis_index("frames")
    r = lax.axis_index("rows")
    above = lax.rem(r + n_rows - 1, n_rows)
    below = lax.rem(r + 1, n_rows)
    peers = [lax.rem(f + d, NF) for d in range(1, NF)]

    barrier = pltpu.get_barrier_semaphore()
    for p in peers:
        pl.semaphore_signal(barrier, inc=1, device_id={"frames": p}, device_id_type=MESH)
    for p in (above, below):
        pl.semaphore_signal(barrier, inc=1, device_id={"rows": p}, device_id_type=MESH)

    loads = [
        pltpu.make_async_copy(a, b, load_sem.at[i])
        for i, (a, b) in enumerate(
            (
                (series, series_v),
                (mix, mix_v),
                (lift4, lift4_v),
                (place, place_v),
                (fwd, fwd_v),
                (inv, inv_v),
                (lift_bias, lift_bias_v),
                (mix_bias, mix_bias_v),
                (proj, proj_v),
                (proj_bias, proj_bias_v),
            )
        )
    ]
    for c in loads:
        c.start()

    loads[0].wait()
    for ri in range(2):
        series_f[ri] = series_v[:, 0, :, ri * 128 : ri * 128 + 128].astype(F32).reshape(T * R, 128)
    for ri in range(2):
        parts = [series_f[ri, pl.ds(i, T, stride=R), :] for i in range(R)]
        for i, part in enumerate(butterfly(parts)):
            sent[i, ri * T : ri * T + T, :] = part.astype(BF16)

    pl.semaphore_wait(barrier, NF + 1)
    first = [
        pltpu.make_async_remote_copy(
            src_ref=sent.at[p],
            dst_ref=got.at[f],
            send_sem=send_sem.at[i],
            recv_sem=recv_sem.at[i],
            device_id={"frames": p},
            device_id_type=MESH,
        )
        for i, p in enumerate(peers)
    ]
    for c in first:
        c.start()
    got[f] = sent[f]

    for c in loads[1:]:
        c.wait()
    for q in range(G // KB):
        lift_m[:, q * 256 : q * 256 + 256] = jnp.dot(
            place_v[q], lift4_v[...], preferred_element_type=F32
        ).astype(BF16)
    zero = jnp.zeros((O, O), BF16)
    for b in range(3):
        t0, t1, t2 = (mix_v[a, b] for a in range(3))
        rows = (
            (t1, t0, zero, zero),
            (t2, t1, t0, zero),
            (zero, t2, t1, t0),
            (zero, zero, t2, t1),
        )
        for j, row in enumerate(rows):
            mix_m[b * 256 + j * O : b * 256 + j * O + O, :] = jnp.concatenate(row, axis=1)
        mix_m[768 + b * 128 : 768 + b * 128 + O, :] = jnp.concatenate((zero, zero, zero, t2), axis=1)
        mix_m[768 + b * 128 + O : 768 + b * 128 + 128, :] = jnp.concatenate((t0, zero, zero, zero), axis=1)
    hid[0] = jnp.zeros(hid.shape[1:], BF16)
    hid[NB + 1] = jnp.zeros(hid.shape[1:], BF16)

    for c in first:
        c.wait_recv()
    xt[...] = got[...].reshape(256, 128).T

    halos = [
        pltpu.make_async_remote_copy(
            src_ref=xt.at[pl.ds(lo, 2 * C)],
            dst_ref=halo.at[i],
            send_sem=halo_send_sem.at[i],
            recv_sem=halo_recv_sem.at[i],
            device_id={"rows": p},
            device_id_type=MESH,
        )
        for i, (lo, p) in enumerate(((6 * C, below), (0, above)))
    ]
    for c in halos:
        c.start()

    own = jnp.dot(xt[...], fwd_v[...], preferred_element_type=F32).astype(BF16)
    for g in range(NG):
        spec[g, 2 * C : 10 * C, :] = own[:, g * 128 : g * 128 + 128]

    def gather(g, lo, size):
        lane = lax.broadcasted_iota(jnp.int32, (size, 128), 1)
        rows = [spec[g, lo + b * C : lo + b * C + size, :] for b in range(3)]
        return jnp.where(lane < 2 * W, rows[0], jnp.where(lane < 4 * W, rows[1], rows[2]))

    def lift(patch):
        return [
            jnp.maximum(
                jnp.dot(patch, lift_m[:, q * 256 : q * 256 + 256], preferred_element_type=F32)
                + lift_bias_v[:, q * 256 : q * 256 + 256],
                0.0,
            )
            for q in range(G // KB)
        ]

    for g in range(NG):
        for q, h in enumerate(lift(gather(g, 2 * C, 6 * C))):
            hid[g * KB + q + 1, 2 * C : 8 * C, :] = h.astype(BF16)

    for c in halos:
        c.wait_recv()
    top = jnp.where(r > 0, halo[0], jnp.zeros_like(halo[0]))
    bottom = jnp.where(r < n_rows - 1, halo[1], jnp.zeros_like(halo[1]))
    outer = jnp.dot(
        jnp.concatenate((top, bottom), axis=0), fwd_v[...], preferred_element_type=F32
    ).astype(BF16)
    for g in range(NG):
        spec[g, : 2 * C, :] = outer[: 2 * C, g * 128 : g * 128 + 128]
        spec[g, 10 * C :, :] = outer[2 * C :, g * 128 : g * 128 + 128]

    row = lax.broadcasted_iota(jnp.int32, (4 * C, 256), 0)
    keep = ((row >= C) | (r > 0)) & ((row < 3 * C) | (r < n_rows - 1))
    for g in range(NG):
        patch = jnp.concatenate((gather(g, 0, 2 * C), gather(g, 8 * C, 2 * C)), axis=0)
        for q, h in enumerate(lift(patch)):
            h = jnp.where(keep, h, 0.0).astype(BF16)
            hid[g * KB + q + 1, : 2 * C, :] = h[: 2 * C]
            hid[g * KB + q + 1, 8 * C :, :] = h[2 * C :]

    lane = lax.broadcasted_iota(jnp.int32, (10 * C, 128), 1)

    def block(g, carry):
        total = None
        edges = []
        for q in range(KB):
            kb = g * KB + q + 1
            edges.append(
                jnp.where(lane < O, hid[kb + 1, :, :128], hid[kb - 1, :, 128:])
            )
        for b in range(3):
            rows = jnp.concatenate(
                [hid[g * KB + q + 1, b * C : b * C + 8 * C, :] for q in range(KB)], axis=0
            )
            part = jnp.dot(rows, mix_m[b * 256 : b * 256 + 256, :], preferred_element_type=F32)
            total = part if total is None else total + part
        rows = jnp.concatenate(
            [
                jnp.concatenate([e[b * C : b * C + 8 * C] for b in range(3)], axis=1)
                for e in edges
            ],
            axis=0,
        )
        total = total + jnp.dot(rows, mix_m[768:, :], preferred_element_type=F32)
        mixed = jnp.maximum(total + mix_bias_v[...], 0.0).astype(BF16)
        u = lax.dot_general(
            proj_v[...], mixed, (((1,), (1,)), ((), ())), preferred_element_type=F32
        )
        for q in range(KB):
            lo = pl.multiple_of((g * KB + q) * 8, 8)
            upd[pl.ds(lo, 8), :] = u[:, q * 128 : q * 128 + 128] + proj_bias_v[...]
        return carry

    lax.fori_loop(0, NB // KB, block, 0)

    back = jnp.dot(inv_v[...], upd[...].astype(BF16), preferred_element_type=F32)
    sent2[...] = back.astype(BF16).reshape(NF, 2 * T, 128)

    second = [
        pltpu.make_async_remote_copy(
            src_ref=sent2.at[p],
            dst_ref=got2.at[f],
            send_sem=send2_sem.at[i],
            recv_sem=recv2_sem.at[i],
            device_id={"frames": p},
            device_id_type=MESH,
        )
        for i, p in enumerate(peers)
    ]
    for c in second:
        c.start()
    got2[f] = sent2[f]
    for c in first + halos:
        c.wait_send()
    for c in second:
        c.wait_recv()
    for ri in range(2):
        parts = [got2[i, ri * T : ri * T + T, :].astype(F32) for i in range(NF)]
        for i, part in enumerate(butterfly(parts)):
            at = (ri, pl.ds(i, T, stride=R), slice(None))
            out[at] = part + series_f[at]
    for c in second:
        c.wait_send()


def per_device(series, lift_weight, lift_bias, mix_weight, mix_bias, proj_weight, proj_bias):
    n_rows = lax.axis_size("rows")
    lift4 = jnp.pad(lift_weight.reshape(18, O), ((0, 14), (0, 0)))
    eye = jnp.eye(KB, dtype=BF16)
    lift4 = (eye[:, None, :, None] * lift4[None, :, None, :]).reshape(KB * 32, KB * O)
    proj = (eye[:, None, :, None] * proj_weight.T[None, :, None, :]).reshape(KB * 2, KB * O)
    args = (
        series,
        jnp.asarray(forward_table()),
        jnp.asarray(inverse_table()),
        jnp.asarray(place_table()),
        lift4,
        jnp.tile(lift_bias, G)[None],
        mix_weight,
        jnp.tile(mix_bias, KB)[None],
        proj,
        jnp.broadcast_to(jnp.tile(proj_bias, KB)[:, None], (8, 128)),
    )
    scratch = [pltpu.VMEM(a.shape, a.dtype) for a in args]
    scratch[0] = pltpu.VMEM((T, 1, R, 256), BF16)
    out = pl.pallas_call(
        functools.partial(kernel, n_rows),
        out_shape=jax.ShapeDtypeStruct((2, T * R, 128), F32),
        in_specs=[pl.BlockSpec(memory_space=pl.ANY)] * len(args),
        out_specs=pl.BlockSpec(memory_space=pltpu.VMEM),
        scratch_shapes=scratch
        + [
            pltpu.VMEM((2, T * R, 128), F32),
            pltpu.VMEM((NF, 2 * T, 128), BF16),
            pltpu.VMEM((NF, 2 * T, 128), BF16),
            pltpu.VMEM((R * C, 256), BF16),
            pltpu.VMEM((2, 2 * C, 256), BF16),
            pltpu.VMEM((NG, 12 * C, 128), BF16),
            pltpu.VMEM((NG, 6 * C, 128), BF16),
            pltpu.VMEM((NG, 4 * C, 128), BF16),
            pltpu.VMEM((128, G * O), BF16),
            pltpu.VMEM((1152, 256), BF16),
            pltpu.VMEM((NB + 2, 10 * C, 256), BF16),
            pltpu.VMEM((2 * N, 128), F32),
            pltpu.VMEM((NF, 2 * T, 128), BF16),
            pltpu.VMEM((NF, 2 * T, 128), BF16),
            pltpu.SemaphoreType.DMA((len(args),)),
            pltpu.SemaphoreType.DMA((NF - 1,)),
            pltpu.SemaphoreType.DMA((NF - 1,)),
            pltpu.SemaphoreType.DMA((2,)),
            pltpu.SemaphoreType.DMA((2,)),
            pltpu.SemaphoreType.DMA((NF - 1,)),
            pltpu.SemaphoreType.DMA((NF - 1,)),
        ],
        compiler_params=pltpu.CompilerParams(
            collective_id=0, has_side_effects=True, vmem_limit_bytes=40 * 1024 * 1024
        ),
    )(*args)
    return jnp.concatenate((out[0], out[1]), axis=1).reshape(T, 1, R, 256)


def solution(mesh):
    return jax.shard_map(
        per_device,
        mesh=mesh,
        in_specs=(P("frames", None, "rows", None), P(), P(), P(), P(), P(), P()),
        out_specs=P("frames", None, "rows", None),
        check_vma=False,
    )
```

time: 172 us -> 33.7 us (0.20)
  the two profiles are of different devices: /device:TPU:128 before, /device:TPU:2 now
where the time goes in v1:
time: 33.7 us; the launch traced here: 33.4 us
  Pallas kernels  27.5 us (82%)
  local copies, waits for them, and re-layouts  4.99 us (15%)
  other arithmetic  0.87 us (3%)
    pallas_call x1, Pallas kernels, per_device(): pl.pallas_call(functools.partial(kernel, n_rows), out_shape=jax.ShapeDtyp...  27.5 us
    unnamed x20, local copies, waits for them, and re-layouts  4.4 us

profile of v1, /device:TPU:2, one launch (start us, length us, event | category | flops | bytes accessed | tf_op | source)
XLA Modules:
  0.0 33.4 jit_solution(142411336038348102)
XLA Ops:
  0.0 0.0 copy-start.6
  0.0 0.6 %copy-done.6 = f32[64]{0:T(128)S(1)} copy-done((f32[64]{0:T(128)S(1)}, f32[64]{0:T(128)}, u32[]{:S(2)}) %copy-start.6) | copy-done | bytes 280
  0.7 0.0 copy-start.7
  0.7 0.0 copy-start.9
  0.7 0.1 broadcast_in_dim_tile.8.mix_bias
  0.7 0.6 %copy-done.7 = f32[2]{0:T(128)S(1)} copy-done((f32[2]{0:T(128)S(1)}, f32[2]{0:T(128)}, u32[]{:S(2)}) %copy-start.7) | copy-done | bytes 32
  1.3 0.0 copy-start.5
  1.3 0.0 copy-start.8
  1.3 0.1 broadcast_in_dim.4
  1.4 0.0 copy-start.3
  1.4 0.1 broadcast_in_dim.5.proj_bias
  1.5 0.5 %copy-done.5 = bf16[3,3,2,64]{3,2,1,0:T(2,128)(2,1)S(1)} copy-done((bf16[3,3,2,64]{3,2,1,0:T(2,128)(2,1)S(1)}, bf16[3,3,2,64]{3,2,1,0:T(2,128)(2,1)}, u32[]{:S(2)}) %copy-start.5) | copy-done | bytes 2328
  2.0 0.0 copy-done.8
  2.0 0.1 broadcast_multiply_fusion.1
  2.1 0.1 mul.41.proj
  2.2 0.0 copy-done.9
  2.2 0.1 broadcast_in_dim_tile.7.lift_bias
  2.3 0.0 copy-start.1
  2.3 0.1 broadcast_multiply_fusion
  2.4 0.0 copy-start.2
  2.4 0.1 mul.37.lift4
  2.6 0.0 copy-done.3
  2.6 0.6 %copy-done.1 = bf16[3,3,64,64]{3,2,1,0:T(8,128)(2,1)S(1)} copy-done((bf16[3,3,64,64]{3,2,1,0:T(8,128)(2,1)S(1)}, bf16[3,3,64,64]{3,2,1,0:T(8,128)(2,1)}, u32[]{:S(2)}) %copy-start.1) | copy-done | bytes 73752
  3.2 0.1 copy-done.2
  3.3 0.0 copy-start
  3.4 1.0 %copy-done = bf16[256,1024]{1,0:T(8,128)(2,1)S(1)} copy-done((bf16[256,1024]{1,0:T(8,128)(2,1)S(1)}, bf16[256,1024]{1,0:T(8,128)(2,1)}, u32[]{:S(2)}) %copy-start) | copy-done | bytes 524312
  4.4 0.0 copy-start.4
  4.4 0.8 %copy-done.4 = bf16[16,1,8,256]{3,2,1,0:T(8,128)(2,1)S(1)} copy-done((bf16[16,1,8,256]{3,2,1,0:T(8,128)(2,1)S(1)}, bf16[16,1,8,256]{3,2,1,0:T(8,128)(2,1)}, u32[]{:S(2)}) %copy-start.4) | copy-done | bytes 65560
  5.2 27.5 %shard_map.100 = f32[2,128,128]{2,1,0:T(8,128)S(1)} custom-call(bf16[16,1,8,256]{3,2,1,0:T(8,128)(2,1)S(1)} %copy-done.4, bf16[256,1024]{1,0:T(8,128)(2,1)S(1)} %copy-done, bf16[256,256]{1,0:T(8,128)(2,1)S(1)} %copy-done.3, bf16[4,128,128]{2,1,0:T(8,128)(2,1)S(1)} %copy-done.2, bf16[128,256]{1,0:T(8,128)(2,1)S(1)} %mul.37.lift4, ...), custom_call_target="tpu_custom_call" | custom-call | tf_op jit(solution)/shard_map/pallas_call | solution.py:365
  32.8 0.7 %pad_maximum_fusion = f32[16,1,8,256]{3,2,1,0:T(8,128)} fusion(f32[16,1,8,128]{3,2,1,0:T(8,128)S(1)} %get-tuple-element.6, f32[16,1,8,128]{3,2,1,0:T(8,128)S(1)} %get-tuple-element.5), kind=kLoop, calls=%fused_computation | loop fusion | flops 32768 | bytes 262144 | tf_op jit(solution)/shard_map/concatenate | solution.py:398
  (7 shorter events, 0.1 us)
Async XLA Ops:
  0.0 0.7 %copy-start.6 = (f32[64]{0:T(128)S(1)}, f32[64]{0:T(128)}, u32[]{:S(2)}) copy-start(f32[64]{0:T(128)} %param.14) | copy-start | bytes 772
  0.7 0.7 %copy-start.7 = (f32[2]{0:T(128)S(1)}, f32[2]{0:T(128)}, u32[]{:S(2)}) copy-start(f32[2]{0:T(128)} %param.16) | copy-start | bytes 28
  0.7 1.6 %copy-start.9 = (f32[64]{0:T(128)S(1)}, f32[64]{0:T(128)}, u32[]{:S(2)}) copy-start(f32[64]{0:T(128)} %param.12) | copy-start | bytes 772
  1.3 0.7 %copy-start.5 = (bf16[3,3,2,64]{3,2,1,0:T(2,128)(2,1)S(1)}, bf16[3,3,2,64]{3,2,1,0:T(2,128)(2,1)}, u32[]{:S(2)}) copy-start(bf16[3,3,2,64]{3,2,1,0:T(2,128)(2,1)} %param.11) | copy-start | bytes 6916
  1.3 0.7 %copy-start.8 = (bf16[64,2]{0,1:T(2,128)(2,1)S(1)}, bf16[64,2]{0,1:T(2,128)(2,1)}, u32[]{:S(2)}) copy-start(bf16[64,2]{0,1:T(2,128)(2,1)} %param.15) | copy-start | bytes 772
  1.4 1.2 %copy-start.3 = (bf16[256,256]{1,0:T(8,128)(2,1)S(1)}, bf16[256,256]{1,0:T(8,128)(2,1)}, u32[]{:S(2)}) copy-start(bf16[256,256]{1,0:T(8,128)(2,1)} %constant.10.clone.inv) | copy-start | bytes 393220
  2.3 0.9 %copy-start.1 = (bf16[3,3,64,64]{3,2,1,0:T(8,128)(2,1)S(1)}, bf16[3,3,64,64]{3,2,1,0:T(8,128)(2,1)}, u32[]{:S(2)}) copy-start(bf16[3,3,64,64]{3,2,1,0:T(8,128)(2,1)} %mix.1) | copy-start | bytes 221188
  2.4 0.9 %copy-start.2 = (bf16[4,128,128]{2,1,0:T(8,128)(2,1)S(1)}, bf16[4,128,128]{2,1,0:T(8,128)(2,1)}, u32[]{:S(2)}) copy-start(bf16[4,128,128]{2,1,0:T(8,128)(2,1)} %constant.11.clone.place) | copy-start | bytes 393220
  3.3 1.0 %copy-start = (bf16[256,1024]{1,0:T(8,128)(2,1)S(1)}, bf16[256,1024]{1,0:T(8,128)(2,1)}, u32[]{:S(2)}) copy-start(bf16[256,1024]{1,0:T(8,128)(2,1)} %constant.9.clone.fwd) | copy-start | bytes 1572868
  4.4 0.8 %copy-start.4 = (bf16[16,1,8,256]{3,2,1,0:T(8,128)(2,1)S(1)}, bf16[16,1,8,256]{3,2,1,0:T(8,128)(2,1)}, u32[]{:S(2)}) copy-start(bf16[16,1,8,256]{3,2,1,0:T(8,128)(2,1)} %series.1) | copy-start | bytes 196612

commit v2 on v1

--- a/solution.py
+++ b/solution.py
@@ -99,7 +99,7 @@
     fwd,
     inv,
     place,
-    lift4,
+    lift,
     lift_bias,
     mix,
     mix_bias,
@@ -110,7 +110,7 @@
     fwd_v,
     inv_v,
     place_v,
-    lift4_v,
+    lift_v,
     lift_bias_v,
     mix_v,
     mix_bias_v,
@@ -122,8 +122,8 @@
     xt,
     halo,
     spec,
-    patch_a,
-    patch_b,
+    taps,
+    ends,
     lift_m,
     mix_m,
     hid,
@@ -156,7 +156,7 @@
             (
                 (series, series_v),
                 (mix, mix_v),
-                (lift4, lift4_v),
+                (lift, lift_v),
                 (place, place_v),
                 (fwd, fwd_v),
                 (inv, inv_v),
@@ -196,10 +196,37 @@
 
     for c in loads[1:]:
         c.wait()
+    taps[...] = jnp.zeros(taps.shape, F32)
+    for a in range(3):
+        for b in range(3):
+            taps[(a * 3 + b) * 2 : (a * 3 + b) * 2 + 2, :O] = lift_v[a, b].astype(F32)
+    left = taps[...]
+    right = pltpu.roll(left, O, 1)
+    none = jnp.zeros_like(left)
+    lift4 = jnp.concatenate(
+        [jnp.concatenate(p, axis=1) for p in ((left, none), (right, none), (none, left), (none, right))],
+        axis=0,
+    ).astype(BF16)
     for q in range(G // KB):
         lift_m[:, q * 256 : q * 256 + 256] = jnp.dot(
-            place_v[q], lift4_v[...], preferred_element_type=F32
+            place_v[q], lift4, preferred_element_type=F32
         ).astype(BF16)
+    for k in range(KB):
+        ends[k * 2 : k * 2 + 2, :] = proj_v[...].astype(F32)
+    proj4 = jnp.concatenate([ends[...]] * KB, axis=1)
+    proj4 = jnp.where(
+        lax.broadcasted_iota(jnp.int32, proj4.shape, 0) // 2
+        == lax.broadcasted_iota(jnp.int32, proj4.shape, 1) // O,
+        proj4,
+        0.0,
+    ).astype(BF16)
+    lift_bias4 = jnp.concatenate([lift_bias_v[...]] * KB, axis=1)
+    mix_bias4 = jnp.concatenate([mix_bias_v[...]] * KB, axis=1)
+    proj_bias4 = jnp.where(
+        lax.broadcasted_iota(jnp.int32, (8, 128), 0) % 2 == 0,
+        jnp.broadcast_to(proj_bias_v[:, :1], (8, 128)),
+        jnp.broadcast_to(proj_bias_v[:, 1:], (8, 128)),
+    )
     zero = jnp.zeros((O, O), BF16)
     for b in range(3):
         t0, t1, t2 = (mix_v[a, b] for a in range(3))
@@ -243,18 +270,18 @@
         rows = [spec[g, lo + b * C : lo + b * C + size, :] for b in range(3)]
         return jnp.where(lane < 2 * W, rows[0], jnp.where(lane < 4 * W, rows[1], rows[2]))
 
-    def lift(patch):
+    def lifted(patch):
         return [
             jnp.maximum(
                 jnp.dot(patch, lift_m[:, q * 256 : q * 256 + 256], preferred_element_type=F32)
-                + lift_bias_v[:, q * 256 : q * 256 + 256],
+                + lift_bias4,
                 0.0,
             )
             for q in range(G // KB)
         ]
 
     for g in range(NG):
-        for q, h in enumerate(lift(gather(g, 2 * C, 6 * C))):
+        for q, h in enumerate(lifted(gather(g, 2 * C, 6 * C))):
             hid[g * KB + q + 1, 2 * C : 8 * C, :] = h.astype(BF16)
 
     for c in halos:
@@ -272,45 +299,23 @@
     keep = ((row >= C) | (r > 0)) & ((row < 3 * C) | (r < n_rows - 1))
     for g in range(NG):
         patch = jnp.concatenate((gather(g, 0, 2 * C), gather(g, 8 * C, 2 * C)), axis=0)
-        for q, h in enumerate(lift(patch)):
+        for q, h in enumerate(lifted(patch)):
             h = jnp.where(keep, h, 0.0).astype(BF16)
             hid[g * KB + q + 1, : 2 * C, :] = h[: 2 * C]
             hid[g * KB + q + 1, 8 * C :, :] = h[2 * C :]
 
-    lane = lax.broadcasted_iota(jnp.int32, (10 * C, 128), 1)
-
-    def block(g, carry):
-        total = None
-        edges = []
-        for q in range(KB):
-            kb = g * KB + q + 1
-            edges.append(
-                jnp.where(lane < O, hid[kb + 1, :, :128], hid[kb - 1, :, 128:])
-            )
-        for b in range(3):
-            rows = jnp.concatenate(
-                [hid[g * KB + q + 1, b * C : b * C + 8 * C, :] for q in range(KB)], axis=0
-            )
-            part = jnp.dot(rows, mix_m[b * 256 : b * 256 + 256, :], preferred_element_type=F32)
-            total = part if total is None else total + part
-        rows = jnp.concatenate(
-            [
-                jnp.concatenate([e[b * C : b * C + 8 * C] for b in range(3)], axis=1)
-                for e in edges
-            ],
-            axis=0,
-        )
-        total = total + jnp.dot(rows, mix_m[768:, :], preferred_element_type=F32)
-        mixed = jnp.maximum(total + mix_bias_v[...], 0.0).astype(BF16)
-        u = lax.dot_general(
-            proj_v[...], mixed, (((1,), (1,)), ((), ())), preferred_element_type=F32
-        )
-        for q in range(KB):
-            lo = pl.multiple_of((g * KB + q) * 8, 8)
-            upd[pl.ds(lo, 8), :] = u[:, q * 128 : q * 128 + 128] + proj_bias_v[...]
-        return carry
-
-    lax.fori_loop(0, NB // KB, block, 0)
+    lane = lax.broadcasted_iota(jnp.int32, (8 * C, 128), 1)
+    rows = []
+    for kb in range(1, NB + 1):
+        taps_b = [pl.ds(b * C, 8 * C) for b in range(3)]
+        main = [hid[kb, at, :] for at in taps_b]
+        edge = [jnp.where(lane < O, hid[kb + 1, at, :128], hid[kb - 1, at, 128:]) for at in taps_b]
+        rows.append(jnp.concatenate(main + edge, axis=1))
+    total = jnp.dot(jnp.concatenate(rows, axis=0), mix_m[...], preferred_element_type=F32)
+    mixed = jnp.maximum(total + mix_bias4, 0.0).astype(BF16)
+    u = lax.dot_general(proj4, mixed, (((1,), (1,)), ((), ())), preferred_element_type=F32)
+    for kb in range(NB):
+        upd[kb * 8 : kb * 8 + 8, :] = u[:, kb * 128 : kb * 128 + 128] + proj_bias4
 
     back = jnp.dot(inv_v[...], upd[...].astype(BF16), preferred_element_type=F32)
     sent2[...] = back.astype(BF16).reshape(NF, 2 * T, 128)
@@ -344,28 +349,23 @@
 
 def per_device(series, lift_weight, lift_bias, mix_weight, mix_bias, proj_weight, proj_bias):
     n_rows = lax.axis_size("rows")
-    lift4 = jnp.pad(lift_weight.reshape(18, O), ((0, 14), (0, 0)))
-    eye = jnp.eye(KB, dtype=BF16)
-    lift4 = (eye[:, None, :, None] * lift4[None, :, None, :]).reshape(KB * 32, KB * O)
-    proj = (eye[:, None, :, None] * proj_weight.T[None, :, None, :]).reshape(KB * 2, KB * O)
     args = (
         series,
         jnp.asarray(forward_table()),
         jnp.asarray(inverse_table()),
         jnp.asarray(place_table()),
-        lift4,
-        jnp.tile(lift_bias, G)[None],
+        lift_weight,
+        lift_bias[None],
         mix_weight,
-        jnp.tile(mix_bias, KB)[None],
-        proj,
-        jnp.broadcast_to(jnp.tile(proj_bias, KB)[:, None], (8, 128)),
+        mix_bias[None],
+        proj_weight.T,
+        proj_bias[None],
     )
     scratch = [pltpu.VMEM(a.shape, a.dtype) for a in args]
-    scratch[0] = pltpu.VMEM((T, 1, R, 256), BF16)
     out = pl.pallas_call(
         functools.partial(kernel, n_rows),
         out_shape=jax.ShapeDtypeStruct((2, T * R, 128), F32),
-        in_specs=[pl.BlockSpec(memory_space=pl.ANY)] * len(args),
+        in_specs=[pl.BlockSpec(memory_space=pltpu.HBM)] * len(args),
         out_specs=pl.BlockSpec(memory_space=pltpu.VMEM),
         scratch_shapes=scratch
         + [
@@ -375,8 +375,8 @@
             pltpu.VMEM((R * C, 256), BF16),
             pltpu.VMEM((2, 2 * C, 256), BF16),
             pltpu.VMEM((NG, 12 * C, 128), BF16),
-            pltpu.VMEM((NG, 6 * C, 128), BF16),
-            pltpu.VMEM((NG, 4 * C, 128), BF16),
+            pltpu.VMEM((32, 128), F32),
+            pltpu.VMEM((8, O), F32),
             pltpu.VMEM((128, G * O), BF16),
             pltpu.VMEM((1152, 256), BF16),
             pltpu.VMEM((NB + 2, 10 * C, 256), BF16),
@@ -392,7 +392,7 @@
             pltpu.SemaphoreType.DMA((NF - 1,)),
         ],
         compiler_params=pltpu.CompilerParams(
-            collective_id=0, has_side_effects=True, vmem_limit_bytes=40 * 1024 * 1024
+            collective_id=0, has_side_effects=True, vmem_limit_bytes=58 * 1024 * 1024
         ),
     )(*args)
     return jnp.concatenate((out[0], out[1]), axis=1).reshape(T, 1, R, 256)

time: 33.7 us -> 28.8 us (0.85)
  local copies, waits for them, and re-layouts: 4.99 us -> 0.88 us
  Pallas kernels: 27.5 us -> 27.1 us
    unnamed x20 -> x0, local copies, waits for them, and re-layouts: 4.4 us -> none
    concatenate x1, local copies, waits for them, and re-layouts: 0.01 us -> 0.88 us  [per_device(): return jnp.concatenate((out[0], out[1]), axis=1).reshape(T, 1, R, 256)]
    pallas_call x1, Pallas kernels: 27.5 us -> 27.1 us  [per_device(): pl.pallas_call(functools.partial(kernel, n_rows), out_shape=jax.ShapeDtyp...]
where the time goes in v2:
time: 28.8 us; the launch traced here: 28.7 us
  Pallas kernels  27.1 us (94%)
  local copies, waits for them, and re-layouts  0.88 us (3%)
  other arithmetic  0.67 us (2%)
    pallas_call x1, Pallas kernels, per_device(): pl.pallas_call(functools.partial(kernel, n_rows), out_shape=jax.ShapeDtyp...  27.1 us
    concatenate x1, local copies, waits for them, and re-layouts, per_device(): return jnp.concatenate((out[0], out[1]), axis=1).reshape(T, 1, R, 256)  0.88 us
    concatenate x1, other arithmetic, per_device(): return jnp.concatenate((out[0], out[1]), axis=1).reshape(T, 1, R, 256)  0.67 us

profile of v2, /device:TPU:2, one launch (start us, length us, event | category | flops | bytes accessed | tf_op | source)
XLA Modules:
  0.0 28.7 jit_solution(607820592100736353)
XLA Ops:
  0.0 27.1 %shard_map.100 = f32[2,128,128]{2,1,0:T(8,128)} custom-call(bf16[16,1,8,256]{3,2,1,0:T(8,128)(2,1)} %series.1, bf16[256,1024]{1,0:T(8,128)(2,1)} %constant.6.clone.fwd, bf16[256,256]{1,0:T(8,128)(2,1)} %constant.7.clone.inv, bf16[4,128,128]{2,1,0:T(8,128)(2,1)} %constant.8.clone.place, bf16[3,3,2,64]{3,2,1,0:T(2,128)(2,1)} %lift.1, f32[1,64]{1,0:T(1,128)} %bitcast.12, ...), custom_call_target="tpu_custom_call" | custom-call | tf_op jit(solution)/shard_map/pallas_call | solution.py:365
  27.1 0.9 %slice_bitcast_fusion.1 = (f32[16,1,8,128]{3,2,1,0:T(8,128)S(1)}, f32[16,1,8,128]{3,2,1,0:T(8,128)S(1)}) fusion(f32[2,128,128]{2,1,0:T(8,128)} %shard_map.100), kind=kLoop, calls=%fused_computation.2 | loop fusion | bytes 262144 | tf_op jit(solution)/shard_map/concatenate | solution.py:398
  28.0 0.7 %pad_maximum_fusion = f32[16,1,8,256]{3,2,1,0:T(8,128)} fusion(f32[16,1,8,128]{3,2,1,0:T(8,128)S(1)} %get-tuple-element.6, f32[16,1,8,128]{3,2,1,0:T(8,128)S(1)} %get-tuple-element.5), kind=kLoop, calls=%fused_computation | loop fusion | flops 32768 | bytes 262144 | tf_op jit(solution)/shard_map/concatenate | solution.py:398

commit v3 on v2

--- a/solution.py
+++ b/solution.py
@@ -75,6 +75,16 @@
                     for i in range(2):
                         full[q, b * 2 * W + (q * KB + j + a) * 2 + i, j, (a * 3 + b) * 2 + i] = 1
     return full.reshape(G // KB, 128, 128).astype(ml_dtypes.bfloat16)
+
+
+PARTNERS = (5, 7, 3, 1, 4, 6, 2)
+
+
+def partner(f, m):
+    for bit in range(3):
+        if m >> bit & 1:
+            f = f + (1 << bit) * (1 - 2 * (f // (1 << bit) % 2))
+    return f
 
 
 def butterfly(parts):
@@ -127,7 +137,7 @@
     lift_m,
     mix_m,
     hid,
-    upd,
+    mixed,
     sent2,
     got2,
     load_sem,
@@ -142,13 +152,21 @@
     r = lax.axis_index("rows")
     above = lax.rem(r + n_rows - 1, n_rows)
     below = lax.rem(r + 1, n_rows)
-    peers = [lax.rem(f + d, NF) for d in range(1, NF)]
+    has_above = r > 0
+    has_below = r < n_rows - 1
+    peers = [partner(f, m) for m in PARTNERS]
 
     barrier = pltpu.get_barrier_semaphore()
     for p in peers:
         pl.semaphore_signal(barrier, inc=1, device_id={"frames": p}, device_id_type=MESH)
-    for p in (above, below):
-        pl.semaphore_signal(barrier, inc=1, device_id={"rows": p}, device_id_type=MESH)
+
+    @pl.when(has_above)
+    def _():
+        pl.semaphore_signal(barrier, inc=1, device_id={"rows": above}, device_id_type=MESH)
+
+    @pl.when(has_below)
+    def _():
+        pl.semaphore_signal(barrier, inc=1, device_id={"rows": below}, device_id_type=MESH)
 
     loads = [
         pltpu.make_async_copy(a, b, load_sem.at[i])
@@ -178,7 +196,8 @@
         for i, part in enumerate(butterfly(parts)):
             sent[i, ri * T : ri * T + T, :] = part.astype(BF16)
 
-    pl.semaphore_wait(barrier, NF + 1)
+    neighbours = jnp.where(has_above, 1, 0) + jnp.where(has_below, 1, 0)
+    pl.semaphore_wait(barrier, NF - 1 + neighbours)
     first = [
         pltpu.make_async_remote_copy(
             src_ref=sent.at[p],
@@ -258,66 +277,101 @@
         )
         for i, (lo, p) in enumerate(((6 * C, below), (0, above)))
     ]
-    for c in halos:
-        c.start()
+    down, up = halos
+
+    @pl.when(has_below)
+    def _():
+        down.start()
+
+    @pl.when(has_above)
+    def _():
+        up.start()
+
+    @pl.when(r == 0)
+    def _():
+        halo[0] = jnp.zeros(halo.shape[1:], BF16)
+
+    @pl.when(r == n_rows - 1)
+    def _():
+        halo[1] = jnp.zeros(halo.shape[1:], BF16)
 
     own = jnp.dot(xt[...], fwd_v[...], preferred_element_type=F32).astype(BF16)
     for g in range(NG):
         spec[g, 2 * C : 10 * C, :] = own[:, g * 128 : g * 128 + 128]
 
+    lane = lax.broadcasted_iota(jnp.int32, (10 * C, 128), 1)
+
     def gather(g, lo, size):
-        lane = lax.broadcasted_iota(jnp.int32, (size, 128), 1)
         rows = [spec[g, lo + b * C : lo + b * C + size, :] for b in range(3)]
-        return jnp.where(lane < 2 * W, rows[0], jnp.where(lane < 4 * W, rows[1], rows[2]))
-
-    def lifted(patch):
-        return [
-            jnp.maximum(
-                jnp.dot(patch, lift_m[:, q * 256 : q * 256 + 256], preferred_element_type=F32)
-                + lift_bias4,
-                0.0,
-            )
-            for q in range(G // KB)
-        ]
-
-    for g in range(NG):
-        for q, h in enumerate(lifted(gather(g, 2 * C, 6 * C))):
-            hid[g * KB + q + 1, 2 * C : 8 * C, :] = h.astype(BF16)
-
-    for c in halos:
-        c.wait_recv()
-    top = jnp.where(r > 0, halo[0], jnp.zeros_like(halo[0]))
-    bottom = jnp.where(r < n_rows - 1, halo[1], jnp.zeros_like(halo[1]))
+        at = lane[:size]
+        return jnp.where(at < 2 * W, rows[0], jnp.where(at < 4 * W, rows[1], rows[2]))
+
+    def lift_rows(parts):
+        size = sum(n for _, n in parts)
+        patch = jnp.concatenate([gather(g, lo, n) for g in range(NG) for lo, n in parts], axis=0)
+        for q in range(G // KB):
+            h = jnp.dot(patch, lift_m[:, q * 256 : q * 256 + 256], preferred_element_type=F32)
+            h = jnp.maximum(h + lift_bias4, 0.0).astype(BF16)
+            for g in range(NG):
+                at = g * size
+                for lo, n in parts:
+                    hid[g * KB + q + 1, lo : lo + n, :] = h[at : at + n]
+                    at += n
+
+    def mix_rows(parts):
+        rows = []
+        for kb in range(1, NB + 1):
+            for lo, n in parts:
+                at = [pl.ds(lo + b * C, n) for b in range(3)]
+                main = [hid[kb, i, :] for i in at]
+                edge = [jnp.where(lane[:n] < O, hid[kb + 1, i, :128], hid[kb - 1, i, 128:]) for i in at]
+                rows.append(jnp.concatenate(main + edge, axis=1))
+        total = jnp.dot(jnp.concatenate(rows, axis=0), mix_m[...], preferred_element_type=F32)
+        total = jnp.maximum(total + mix_bias4, 0.0).astype(BF16)
+        at = 0
+        for kb in range(NB):
+            for lo, n in parts:
+                mixed[kb, lo : lo + n, :] = total[at : at + n]
+                at += n
+
+    lift_rows([(2 * C, 6 * C)])
+    mix_rows([(2 * C, 4 * C)])
+
+    @pl.when(has_above)
+    def _():
+        down.wait_recv()
+
+    @pl.when(has_below)
+    def _():
+        up.wait_recv()
+
     outer = jnp.dot(
-        jnp.concatenate((top, bottom), axis=0), fwd_v[...], preferred_element_type=F32
+        halo[...].reshape(4 * C, 256), fwd_v[...], preferred_element_type=F32
     ).astype(BF16)
     for g in range(NG):
         spec[g, : 2 * C, :] = outer[: 2 * C, g * 128 : g * 128 + 128]
         spec[g, 10 * C :, :] = outer[2 * C :, g * 128 : g * 128 + 128]
-
-    row = lax.broadcasted_iota(jnp.int32, (4 * C, 256), 0)
-    keep = ((row >= C) | (r > 0)) & ((row < 3 * C) | (r < n_rows - 1))
-    for g in range(NG):
-        patch = jnp.concatenate((gather(g, 0, 2 * C), gather(g, 8 * C, 2 * C)), axis=0)
-        for q, h in enumerate(lifted(patch)):
-            h = jnp.where(keep, h, 0.0).astype(BF16)
-            hid[g * KB + q + 1, : 2 * C, :] = h[: 2 * C]
-            hid[g * KB + q + 1, 8 * C :, :] = h[2 * C :]
-
-    lane = lax.broadcasted_iota(jnp.int32, (8 * C, 128), 1)
-    rows = []
-    for kb in range(1, NB + 1):
-        taps_b = [pl.ds(b * C, 8 * C) for b in range(3)]
-        main = [hid[kb, at, :] for at in taps_b]
-        edge = [jnp.where(lane < O, hid[kb + 1, at, :128], hid[kb - 1, at, 128:]) for at in taps_b]
-        rows.append(jnp.concatenate(main + edge, axis=1))
-    total = jnp.dot(jnp.concatenate(rows, axis=0), mix_m[...], preferred_element_type=F32)
-    mixed = jnp.maximum(total + mix_bias4, 0.0).astype(BF16)
-    u = lax.dot_general(proj4, mixed, (((1,), (1,)), ((), ())), preferred_element_type=F32)
-    for kb in range(NB):
-        upd[kb * 8 : kb * 8 + 8, :] = u[:, kb * 128 : kb * 128 + 128] + proj_bias4
-
-    back = jnp.dot(inv_v[...], upd[...].astype(BF16), preferred_element_type=F32)
+    lift_rows([(0, 2 * C), (8 * C, 2 * C)])
+
+    @pl.when(r == 0)
+    def _():
+        hid[:, :C, :] = jnp.zeros((NB + 2, C, 256), BF16)
+
+    @pl.when(r == n_rows - 1)
+    def _():
+        hid[:, 9 * C :, :] = jnp.zeros((NB + 2, C, 256), BF16)
+
+    mix_rows([(0, 2 * C), (6 * C, 2 * C)])
+    u = lax.dot_general(
+        proj4,
+        mixed[...].reshape(NB * 8 * C, 256),
+        (((1,), (1,)), ((), ())),
+        preferred_element_type=F32,
+    )
+    update = jnp.concatenate(
+        [u[:, kb * 128 : kb * 128 + 128] + proj_bias4 for kb in range(NB)], axis=0
+    ).astype(BF16)
+    back = jnp.dot(inv_v[...], update, preferred_element_type=F32)
     sent2[...] = back.astype(BF16).reshape(NF, 2 * T, 128)
 
     second = [
@@ -334,8 +388,6 @@
     for c in second:
         c.start()
     got2[f] = sent2[f]
-    for c in first + halos:
-        c.wait_send()
     for c in second:
         c.wait_recv()
     for ri in range(2):
@@ -343,8 +395,16 @@
         for i, part in enumerate(butterfly(parts)):
             at = (ri, pl.ds(i, T, stride=R), slice(None))
             out[at] = part + series_f[at]
-    for c in second:
+    for c in first + second:
         c.wait_send()
+
+    @pl.when(has_below)
+    def _():
+        down.wait_send()
+
+    @pl.when(has_above)
+    def _():
+        up.wait_send()
 
 
 def per_device(series, lift_weight, lift_bias, mix_weight, mix_bias, proj_weight, proj_bias):
@@ -364,7 +424,7 @@
     scratch = [pltpu.VMEM(a.shape, a.dtype) for a in args]
     out = pl.pallas_call(
         functools.partial(kernel, n_rows),
-        out_shape=jax.ShapeDtypeStruct((2, T * R, 128), F32),
+        out_shape=pltpu.VMEM((2, T * R, 128), F32),
         in_specs=[pl.BlockSpec(memory_space=pltpu.HBM)] * len(args),
         out_specs=pl.BlockSpec(memory_space=pltpu.VMEM),
         scratch_shapes=scratch
@@ -380,7 +440,7 @@
             pltpu.VMEM((128, G * O), BF16),
             pltpu.VMEM((1152, 256), BF16),
             pltpu.VMEM((NB + 2, 10 * C, 256), BF16),
-            pltpu.VMEM((2 * N, 128), F32),
+            pltpu.VMEM((NB, R * C, 256), BF16),
             pltpu.VMEM((NF, 2 * T, 128), BF16),
             pltpu.VMEM((NF, 2 * T, 128), BF16),
             pltpu.SemaphoreType.DMA((len(args),)),
@@ -392,7 +452,7 @@
             pltpu.SemaphoreType.DMA((NF - 1,)),
         ],
         compiler_params=pltpu.CompilerParams(
-            collective_id=0, has_side_effects=True, vmem_limit_bytes=58 * 1024 * 1024
+            collective_id=0, has_side_effects=True, vmem_limit_bytes=56 * 1024 * 1024
         ),
     )(*args)
     return jnp.concatenate((out[0], out[1]), axis=1).reshape(T, 1, R, 256)

time: 28.8 us -> 24.2 us (0.84)
  the two profiles are of different devices: /device:TPU:2 before, /device:TPU:105 now
where the time goes in v3:
time: 24.2 us; the launch traced here: 23.9 us
  Pallas kernels  23.2 us (96%)
  other arithmetic  0.67 us (3%)
    pallas_call x1, Pallas kernels, per_device(): pl.pallas_call(functools.partial(kernel, n_rows), out_shape=pltpu.VMEM((2...  23.2 us
    concatenate x1, other arithmetic, per_device(): return jnp.concatenate((out[0], out[1]), axis=1).reshape(T, 1, R, 256)  0.67 us

profile of v3, /device:TPU:105, one launch (start us, length us, event | category | flops | bytes accessed | tf_op | source)
XLA Modules:
  0.0 23.9 jit_solution(13475566612537863096)
XLA Ops:
  0.0 23.2 %shard_map.100 = f32[2,128,128]{2,1,0:T(8,128)S(1)} custom-call(bf16[16,1,8,256]{3,2,1,0:T(8,128)(2,1)} %series.1, bf16[256,1024]{1,0:T(8,128)(2,1)} %constant.6.clone.fwd, bf16[256,256]{1,0:T(8,128)(2,1)} %constant.7.clone.inv, bf16[4,128,128]{2,1,0:T(8,128)(2,1)} %constant.8.clone.place, bf16[3,3,2,64]{3,2,1,0:T(2,128)(2,1)} %lift.1, f32[1,64]{1,0:T(1,128)} %bitcast.12, ...), custom_call_target="tpu_custom_call" | custom-call | tf_op jit(solution)/shard_map/pallas_call | solution.py:425
  23.2 0.7 %pad_maximum_fusion = f32[16,1,8,256]{3,2,1,0:T(8,128)} fusion(f32[16,1,8,128]{3,2,1,0:T(8,128)S(1)} %get-tuple-element.6, f32[16,1,8,128]{3,2,1,0:T(8,128)S(1)} %get-tuple-element.5), kind=kLoop, calls=%fused_computation | loop fusion | flops 32768 | bytes 262144 | tf_op jit(solution)/shard_map/concatenate | solution.py:458
  (1 shorter events, 0.0 us)

commit v4 on v3

--- a/solution.py
+++ b/solution.py
@@ -353,14 +353,11 @@
         spec[g, 10 * C :, :] = outer[2 * C :, g * 128 : g * 128 + 128]
     lift_rows([(0, 2 * C), (8 * C, 2 * C)])
 
-    @pl.when(r == 0)
-    def _():
-        hid[:, :C, :] = jnp.zeros((NB + 2, C, 256), BF16)
-
-    @pl.when(r == n_rows - 1)
-    def _():
-        hid[:, 9 * C :, :] = jnp.zeros((NB + 2, C, 256), BF16)
-
+    top = jnp.full((C, 256), jnp.where(has_above, 1.0, 0.0), F32).astype(BF16)
+    bottom = jnp.full((C, 256), jnp.where(has_below, 1.0, 0.0), F32).astype(BF16)
+    for kb in range(1, NB + 1):
+        hid[kb, :C, :] = hid[kb, :C, :] * top
+        hid[kb, 9 * C :, :] = hid[kb, 9 * C :, :] * bottom
     mix_rows([(0, 2 * C), (6 * C, 2 * C)])
     u = lax.dot_general(
         proj4,

time: 24.2 us -> 24.1 us (level)
  no operation moved by 1% of the time
where the time goes in v4:
time: 24.1 us; the launch traced here: 23.7 us
  Pallas kernels  23 us (95%)
  other arithmetic  0.67 us (3%)
    pallas_call x1, Pallas kernels, per_device(): pl.pallas_call(functools.partial(kernel, n_rows), out_shape=pltpu.VMEM((2...  23 us
    concatenate x1, other arithmetic, per_device(): return jnp.concatenate((out[0], out[1]), axis=1).reshape(T, 1, R, 256)  0.67 us

profile of v4, /device:TPU:105, one launch (start us, length us, event | category | flops | bytes accessed | tf_op | source)
XLA Modules:
  0.0 23.7 jit_solution(11018835087792646037)
XLA Ops:
  0.0 23.0 %shard_map.100 = f32[2,128,128]{2,1,0:T(8,128)S(1)} custom-call(bf16[16,1,8,256]{3,2,1,0:T(8,128)(2,1)} %series.1, bf16[256,1024]{1,0:T(8,128)(2,1)} %constant.6.clone.fwd, bf16[256,256]{1,0:T(8,128)(2,1)} %constant.7.clone.inv, bf16[4,128,128]{2,1,0:T(8,128)(2,1)} %constant.8.clone.place, bf16[3,3,2,64]{3,2,1,0:T(2,128)(2,1)} %lift.1, f32[1,64]{1,0:T(1,128)} %bitcast.12, ...), custom_call_target="tpu_custom_call" | custom-call | tf_op jit(solution)/shard_map/pallas_call | solution.py:422
  23.1 0.7 %pad_maximum_fusion = f32[16,1,8,256]{3,2,1,0:T(8,128)} fusion(f32[16,1,8,128]{3,2,1,0:T(8,128)S(1)} %get-tuple-element.6, f32[16,1,8,128]{3,2,1,0:T(8,128)S(1)} %get-tuple-element.5), kind=kLoop, calls=%fused_computation | loop fusion | flops 32768 | bytes 262144 | tf_op jit(solution)/shard_map/concatenate | solution.py:455
  (1 shorter events, 0.0 us)

commit v5 on v4

--- a/solution.py
+++ b/solution.py
@@ -48,7 +48,7 @@
                 full[:, 1, :, g, lane] = -b
                 full[:, 0, :, g, lane + 1] = b
                 full[:, 1, :, g, lane + 1] = a
-    return full.reshape(NF * 2 * T, NG * 128).astype(ml_dtypes.bfloat16)
+    return full.transpose(1, 0, 2, 3, 4).reshape(2 * NF * T, NG * 128).astype(ml_dtypes.bfloat16)
 
 
 def inverse_table():
@@ -128,9 +128,10 @@
     proj_bias_v,
     series_f,
     sent,
+    edge,
     got,
+    halo,
     xt,
-    halo,
     spec,
     taps,
     ends,
@@ -160,13 +161,14 @@
     for p in peers:
         pl.semaphore_signal(barrier, inc=1, device_id={"frames": p}, device_id_type=MESH)
 
-    @pl.when(has_above)
-    def _():
-        pl.semaphore_signal(barrier, inc=1, device_id={"rows": above}, device_id_type=MESH)
-
-    @pl.when(has_below)
-    def _():
-        pl.semaphore_signal(barrier, inc=1, device_id={"rows": below}, device_id_type=MESH)
+    for has, near in ((has_above, above), (has_below, below)):
+
+        @pl.when(has)
+        def _():
+            for p in peers + [f]:
+                pl.semaphore_signal(
+                    barrier, inc=1, device_id={"frames": p, "rows": near}, device_id_type=MESH
+                )
 
     loads = [
         pltpu.make_async_copy(a, b, load_sem.at[i])
@@ -191,14 +193,20 @@
     loads[0].wait()
     for ri in range(2):
         series_f[ri] = series_v[:, 0, :, ri * 128 : ri * 128 + 128].astype(F32).reshape(T * R, 128)
-    for ri in range(2):
-        parts = [series_f[ri, pl.ds(i, T, stride=R), :] for i in range(R)]
-        for i, part in enumerate(butterfly(parts)):
-            sent[i, ri * T : ri * T + T, :] = part.astype(BF16)
+    tiles = [
+        butterfly([series_f[ri, pl.ds(i, T, stride=R), :] for i in range(R)]) for ri in range(2)
+    ]
+    quarter = lax.broadcasted_iota(jnp.int32, (T, 128), 1) // (2 * C)
+    for i, (re, im) in enumerate(zip(*tiles)):
+        sent[i, :T, :] = re.astype(BF16)
+        sent[i, T:, :] = im.astype(BF16)
+        low = jnp.where(quarter == 0, re, pltpu.roll(im, 2 * C, 1))
+        high = jnp.where(quarter == 2, pltpu.roll(re, 128 - 2 * C, 1), im)
+        edge[i] = jnp.where(quarter < 2, low, high).astype(BF16)
 
     neighbours = jnp.where(has_above, 1, 0) + jnp.where(has_below, 1, 0)
-    pl.semaphore_wait(barrier, NF - 1 + neighbours)
-    first = [
+    pl.semaphore_wait(barrier, NF - 1 + NF * neighbours)
+    own = [
         pltpu.make_async_remote_copy(
             src_ref=sent.at[p],
             dst_ref=got.at[f],
@@ -209,9 +217,43 @@
         )
         for i, p in enumerate(peers)
     ]
-    for c in first:
+    down, up = (
+        [
+            pltpu.make_async_remote_copy(
+                src_ref=edge.at[p],
+                dst_ref=halo.at[side, f],
+                send_sem=halo_send_sem.at[side, i],
+                recv_sem=halo_recv_sem.at[side, i],
+                device_id={"frames": p, "rows": near},
+                device_id_type=MESH,
+            )
+            for i, p in enumerate(peers + [f])
+        ]
+        for side, near in ((0, below), (1, above))
+    )
+
+    for c in own:
         c.start()
+
+    @pl.when(has_below)
+    def _():
+        for c in down:
+            c.start()
+
+    @pl.when(has_above)
+    def _():
+        for c in up:
+            c.start()
+
     got[f] = sent[f]
+
+    @pl.when(r == 0)
+    def _():
+        halo[0] = jnp.zeros(halo.shape[1:], BF16)
+
+    @pl.when(r == n_rows - 1)
+    def _():
+        halo[1] = jnp.zeros(halo.shape[1:], BF16)
 
     for c in loads[1:]:
         c.wait()
@@ -262,42 +304,29 @@
     hid[0] = jnp.zeros(hid.shape[1:], BF16)
     hid[NB + 1] = jnp.zeros(hid.shape[1:], BF16)
 
-    for c in first:
+    for c in own:
         c.wait_recv()
-    xt[...] = got[...].reshape(256, 128).T
-
-    halos = [
-        pltpu.make_async_remote_copy(
-            src_ref=xt.at[pl.ds(lo, 2 * C)],
-            dst_ref=halo.at[i],
-            send_sem=halo_send_sem.at[i],
-            recv_sem=halo_recv_sem.at[i],
-            device_id={"rows": p},
-            device_id_type=MESH,
-        )
-        for i, (lo, p) in enumerate(((6 * C, below), (0, above)))
-    ]
-    down, up = halos
+
+    @pl.when(has_above)
+    def _():
+        for c in down:
+            c.wait_recv()
 
     @pl.when(has_below)
     def _():
-        down.start()
-
-    @pl.when(has_above)
-    def _():
-        up.start()
-
-    @pl.when(r == 0)
-    def _():
-        halo[0] = jnp.zeros(halo.shape[1:], BF16)
-
-    @pl.when(r == n_rows - 1)
-    def _():
-        halo[1] = jnp.zeros(halo.shape[1:], BF16)
-
-    own = jnp.dot(xt[...], fwd_v[...], preferred_element_type=F32).astype(BF16)
+        for c in up:
+            c.wait_recv()
+
+    quarter = lax.broadcasted_iota(jnp.int32, (NF * T, 128), 1) // (2 * C)
+    near = jnp.where(quarter < 2, halo[1].reshape(NF * T, 128), halo[0].reshape(NF * T, 128)).T
+    for ri in range(2):
+        at = slice(ri * 128, ri * 128 + 128)
+        xt[: 2 * C, at] = near[(2 + ri) * 2 * C : (3 + ri) * 2 * C]
+        xt[2 * C : 10 * C, at] = got[:, ri * T : ri * T + T, :].reshape(NF * T, 128).T
+        xt[10 * C :, at] = near[ri * 2 * C : (1 + ri) * 2 * C]
+    spectrum = jnp.dot(xt[...], fwd_v[...], preferred_element_type=F32).astype(BF16)
     for g in range(NG):
-        spec[g, 2 * C : 10 * C, :] = own[:, g * 128 : g * 128 + 128]
+        spec[g] = spectrum[:, g * 128 : g * 128 + 128]
 
     lane = lax.broadcasted_iota(jnp.int32, (10 * C, 128), 1)
 
@@ -324,8 +353,8 @@
             for lo, n in parts:
                 at = [pl.ds(lo + b * C, n) for b in range(3)]
                 main = [hid[kb, i, :] for i in at]
-                edge = [jnp.where(lane[:n] < O, hid[kb + 1, i, :128], hid[kb - 1, i, 128:]) for i in at]
-                rows.append(jnp.concatenate(main + edge, axis=1))
+                side = [jnp.where(lane[:n] < O, hid[kb + 1, i, :128], hid[kb - 1, i, 128:]) for i in at]
+                rows.append(jnp.concatenate(main + side, axis=1))
         total = jnp.dot(jnp.concatenate(rows, axis=0), mix_m[...], preferred_element_type=F32)
         total = jnp.maximum(total + mix_bias4, 0.0).astype(BF16)
         at = 0
@@ -334,31 +363,13 @@
                 mixed[kb, lo : lo + n, :] = total[at : at + n]
                 at += n
 
-    lift_rows([(2 * C, 6 * C)])
-    mix_rows([(2 * C, 4 * C)])
-
-    @pl.when(has_above)
-    def _():
-        down.wait_recv()
-
-    @pl.when(has_below)
-    def _():
-        up.wait_recv()
-
-    outer = jnp.dot(
-        halo[...].reshape(4 * C, 256), fwd_v[...], preferred_element_type=F32
-    ).astype(BF16)
-    for g in range(NG):
-        spec[g, : 2 * C, :] = outer[: 2 * C, g * 128 : g * 128 + 128]
-        spec[g, 10 * C :, :] = outer[2 * C :, g * 128 : g * 128 + 128]
-    lift_rows([(0, 2 * C), (8 * C, 2 * C)])
-
+    lift_rows([(0, 10 * C)])
     top = jnp.full((C, 256), jnp.where(has_above, 1.0, 0.0), F32).astype(BF16)
     bottom = jnp.full((C, 256), jnp.where(has_below, 1.0, 0.0), F32).astype(BF16)
     for kb in range(1, NB + 1):
         hid[kb, :C, :] = hid[kb, :C, :] * top
         hid[kb, 9 * C :, :] = hid[kb, 9 * C :, :] * bottom
-    mix_rows([(0, 2 * C), (6 * C, 2 * C)])
+    mix_rows([(0, 8 * C)])
     u = lax.dot_general(
         proj4,
         mixed[...].reshape(NB * 8 * C, 256),
@@ -392,16 +403,18 @@
         for i, part in enumerate(butterfly(parts)):
             at = (ri, pl.ds(i, T, stride=R), slice(None))
             out[at] = part + series_f[at]
-    for c in first + second:
+    for c in own + second:
         c.wait_send()
 
     @pl.when(has_below)
     def _():
-        down.wait_send()
+        for c in down:
+            c.wait_send()
 
     @pl.when(has_above)
     def _():
-        up.wait_send()
+        for c in up:
+            c.wait_send()
 
 
 def per_device(series, lift_weight, lift_bias, mix_weight, mix_bias, proj_weight, proj_bias):
@@ -428,9 +441,10 @@
         + [
             pltpu.VMEM((2, T * R, 128), F32),
             pltpu.VMEM((NF, 2 * T, 128), BF16),
+            pltpu.VMEM((NF, T, 128), BF16),
             pltpu.VMEM((NF, 2 * T, 128), BF16),
-            pltpu.VMEM((R * C, 256), BF16),
-            pltpu.VMEM((2, 2 * C, 256), BF16),
+            pltpu.VMEM((2, NF, T, 128), BF16),
+            pltpu.VMEM((12 * C, 256), BF16),
             pltpu.VMEM((NG, 12 * C, 128), BF16),
             pltpu.VMEM((32, 128), F32),
             pltpu.VMEM((8, O), F32),
@@ -443,8 +457,8 @@
             pltpu.SemaphoreType.DMA((len(args),)),
             pltpu.SemaphoreType.DMA((NF - 1,)),
             pltpu.SemaphoreType.DMA((NF - 1,)),
-            pltpu.SemaphoreType.DMA((2,)),
-            pltpu.SemaphoreType.DMA((2,)),
+            pltpu.SemaphoreType.DMA((2, NF)),
+            pltpu.SemaphoreType.DMA((2, NF)),
             pltpu.SemaphoreType.DMA((NF - 1,)),
             pltpu.SemaphoreType.DMA((NF - 1,)),
         ],

time: 24.1 us -> 23.2 us (0.963); the launches traced: 23.7 us -> 23.1 us
  Pallas kernels: 23 us -> 22.4 us
    pallas_call x1, Pallas kernels: 23 us -> 22.4 us  [per_device(): pl.pallas_call(functools.partial(kernel, n_rows), out_shape=pltpu.VMEM((2...]
where the time goes in v5:
time: 23.2 us; the launch traced here: 23.1 us
  Pallas kernels  22.4 us (97%)
  other arithmetic  0.67 us (3%)
    pallas_call x1, Pallas kernels, per_device(): pl.pallas_call(functools.partial(kernel, n_rows), out_shape=pltpu.VMEM((2...  22.4 us
    concatenate x1, other arithmetic, per_device(): return jnp.concatenate((out[0], out[1]), axis=1).reshape(T, 1, R, 256)  0.67 us

profile of v5, /device:TPU:105, one launch (start us, length us, event | category | flops | bytes accessed | tf_op | source)
XLA Modules:
  0.0 23.1 jit_solution(8389042975176524269)
XLA Ops:
  0.0 22.4 %shard_map.100 = f32[2,128,128]{2,1,0:T(8,128)S(1)} custom-call(bf16[16,1,8,256]{3,2,1,0:T(8,128)(2,1)} %series.1, bf16[256,1024]{1,0:T(8,128)(2,1)} %constant.6.clone.fwd, bf16[256,256]{1,0:T(8,128)(2,1)} %constant.7.clone.inv, bf16[4,128,128]{2,1,0:T(8,128)(2,1)} %constant.8.clone.place, bf16[3,3,2,64]{3,2,1,0:T(2,128)(2,1)} %lift.1, f32[1,64]{1,0:T(1,128)} %bitcast.12, ...), custom_call_target="tpu_custom_call" | custom-call | tf_op jit(solution)/shard_map/pallas_call | solution.py:435
  22.5 0.7 %pad_maximum_fusion = f32[16,1,8,256]{3,2,1,0:T(8,128)} fusion(f32[16,1,8,128]{3,2,1,0:T(8,128)S(1)} %get-tuple-element.6, f32[16,1,8,128]{3,2,1,0:T(8,128)S(1)} %get-tuple-element.5), kind=kLoop, calls=%fused_computation | loop fusion | flops 32768 | bytes 262144 | tf_op jit(solution)/shard_map/concatenate | solution.py:469
  (1 shorter events, 0.0 us)

commit v6 on v5

--- a/solution.py
+++ b/solution.py
@@ -21,7 +21,6 @@
 C = 16
 O = 64
 KB = 4
-NB = N // KB
 G = 16
 NG = N // G
 W = G + 2
@@ -138,7 +137,6 @@
     lift_m,
     mix_m,
     hid,
-    mixed,
     sent2,
     got2,
     load_sem,
@@ -275,11 +273,9 @@
     for k in range(KB):
         ends[k * 2 : k * 2 + 2, :] = proj_v[...].astype(F32)
     proj4 = jnp.concatenate([ends[...]] * KB, axis=1)
+    pair = lax.broadcasted_iota(jnp.int32, proj4.shape, 1) // O
     proj4 = jnp.where(
-        lax.broadcasted_iota(jnp.int32, proj4.shape, 0) // 2
-        == lax.broadcasted_iota(jnp.int32, proj4.shape, 1) // O,
-        proj4,
-        0.0,
+        lax.broadcasted_iota(jnp.int32, proj4.shape, 0) // 2 == pair % 2 * 2 + pair // 2, proj4, 0.0
     ).astype(BF16)
     lift_bias4 = jnp.concatenate([lift_bias_v[...]] * KB, axis=1)
     mix_bias4 = jnp.concatenate([mix_bias_v[...]] * KB, axis=1)
@@ -289,20 +285,23 @@
         jnp.broadcast_to(proj_bias_v[:, 1:], (8, 128)),
     )
     zero = jnp.zeros((O, O), BF16)
-    for b in range(3):
-        t0, t1, t2 = (mix_v[a, b] for a in range(3))
+    for w in range(4):
+
+        def taps_of(a):
+            return tuple(mix_v[a, w - r2] if 0 <= w - r2 <= 2 else zero for r2 in range(2))
+
+        blank = (zero, zero)
         rows = (
-            (t1, t0, zero, zero),
-            (t2, t1, t0, zero),
-            (zero, t2, t1, t0),
-            (zero, zero, t2, t1),
+            taps_of(1) + taps_of(0),
+            taps_of(2) + taps_of(1),
+            blank + taps_of(2),
+            taps_of(0) + blank,
         )
         for j, row in enumerate(rows):
-            mix_m[b * 256 + j * O : b * 256 + j * O + O, :] = jnp.concatenate(row, axis=1)
-        mix_m[768 + b * 128 : 768 + b * 128 + O, :] = jnp.concatenate((zero, zero, zero, t2), axis=1)
-        mix_m[768 + b * 128 + O : 768 + b * 128 + 128, :] = jnp.concatenate((t0, zero, zero, zero), axis=1)
+            at = w * 256 + j * O
+            mix_m[at : at + O, :] = jnp.concatenate(row, axis=1)
     hid[0] = jnp.zeros(hid.shape[1:], BF16)
-    hid[NB + 1] = jnp.zeros(hid.shape[1:], BF16)
+    hid[N // 2 + 1] = jnp.zeros(hid.shape[1:], BF16)
 
     for c in own:
         c.wait_recv()
@@ -330,55 +329,46 @@
 
     lane = lax.broadcasted_iota(jnp.int32, (10 * C, 128), 1)
 
-    def gather(g, lo, size):
-        rows = [spec[g, lo + b * C : lo + b * C + size, :] for b in range(3)]
-        at = lane[:size]
-        return jnp.where(at < 2 * W, rows[0], jnp.where(at < 4 * W, rows[1], rows[2]))
-
-    def lift_rows(parts):
-        size = sum(n for _, n in parts)
-        patch = jnp.concatenate([gather(g, lo, n) for g in range(NG) for lo, n in parts], axis=0)
-        for q in range(G // KB):
-            h = jnp.dot(patch, lift_m[:, q * 256 : q * 256 + 256], preferred_element_type=F32)
-            h = jnp.maximum(h + lift_bias4, 0.0).astype(BF16)
-            for g in range(NG):
-                at = g * size
-                for lo, n in parts:
-                    hid[g * KB + q + 1, lo : lo + n, :] = h[at : at + n]
-                    at += n
-
-    def mix_rows(parts):
-        rows = []
-        for kb in range(1, NB + 1):
-            for lo, n in parts:
-                at = [pl.ds(lo + b * C, n) for b in range(3)]
-                main = [hid[kb, i, :] for i in at]
-                side = [jnp.where(lane[:n] < O, hid[kb + 1, i, :128], hid[kb - 1, i, 128:]) for i in at]
-                rows.append(jnp.concatenate(main + side, axis=1))
-        total = jnp.dot(jnp.concatenate(rows, axis=0), mix_m[...], preferred_element_type=F32)
-        total = jnp.maximum(total + mix_bias4, 0.0).astype(BF16)
-        at = 0
-        for kb in range(NB):
-            for lo, n in parts:
-                mixed[kb, lo : lo + n, :] = total[at : at + n]
-                at += n
-
-    lift_rows([(0, 10 * C)])
-    top = jnp.full((C, 256), jnp.where(has_above, 1.0, 0.0), F32).astype(BF16)
-    bottom = jnp.full((C, 256), jnp.where(has_below, 1.0, 0.0), F32).astype(BF16)
-    for kb in range(1, NB + 1):
-        hid[kb, :C, :] = hid[kb, :C, :] * top
-        hid[kb, 9 * C :, :] = hid[kb, 9 * C :, :] * bottom
-    mix_rows([(0, 8 * C)])
+    patch = []
+    for g in range(NG):
+        rows = [spec[g, b * C : b * C + 10 * C, :] for b in range(3)]
+        patch.append(jnp.where(lane < 2 * W, rows[0], jnp.where(lane < 4 * W, rows[1], rows[2])))
+    patch = jnp.concatenate(patch, axis=0)
+    top = jnp.full((C, 128), jnp.where(has_above, 1.0, 0.0), F32).astype(BF16)
+    bottom = jnp.full((C, 128), jnp.where(has_below, 1.0, 0.0), F32).astype(BF16)
+    for q in range(G // KB):
+        h = jnp.dot(patch, lift_m[:, q * 256 : q * 256 + 256], preferred_element_type=F32)
+        h = jnp.maximum(h + lift_bias4, 0.0).astype(BF16)
+        for g in range(NG):
+            at = g * 10 * C
+            for half in range(2):
+                kp = (g * KB + q) * 2 + half + 1
+                cols = slice(half * 128, half * 128 + 128)
+                hid[kp, :C, :] = h[at : at + C, cols] * top
+                hid[kp, C : 9 * C, :] = h[at + C : at + 9 * C, cols]
+                hid[kp, 9 * C :, :] = h[at + 9 * C : at + 10 * C, cols] * bottom
+
+    blocks = []
+    for kp in range(1, N // 2 + 1):
+        here = hid[kp]
+        beside = jnp.where(lane < O, hid[kp + 1], hid[kp - 1])
+        for rp in range(R // 2):
+            window = [slice((2 * rp + w) * C, (2 * rp + w + 1) * C) for w in range(4)]
+            blocks.append(jnp.concatenate([x[at] for at in window for x in (here, beside)], axis=1))
+    mixed = jnp.dot(jnp.concatenate(blocks, axis=0), mix_m[...], preferred_element_type=F32)
+    mixed = jnp.maximum(mixed + mix_bias4, 0.0).astype(BF16)
     u = lax.dot_general(
-        proj4,
-        mixed[...].reshape(NB * 8 * C, 256),
-        (((1,), (1,)), ((), ())),
-        preferred_element_type=F32,
-    )
-    update = jnp.concatenate(
-        [u[:, kb * 128 : kb * 128 + 128] + proj_bias4 for kb in range(NB)], axis=0
-    ).astype(BF16)
+        proj4, mixed, (((1,), (1,)), ((), ())), preferred_element_type=F32
+    )
+    stay = (lax.broadcasted_iota(jnp.int32, (8, 128), 0) < 4) == (
+        lax.broadcasted_iota(jnp.int32, (8, 128), 1) < 64
+    )
+    update = []
+    for i in range(N // 4):
+        v = u[:, i * 128 : i * 128 + 128]
+        v = jnp.where(stay, v, pltpu.roll(pltpu.roll(v, 4, 0), 64, 1))
+        update.append(v + proj_bias4)
+    update = jnp.concatenate(update, axis=0).astype(BF16)
     back = jnp.dot(inv_v[...], update, preferred_element_type=F32)
     sent2[...] = back.astype(BF16).reshape(NF, 2 * T, 128)
 
@@ -401,7 +391,8 @@
     for ri in range(2):
         parts = [got2[i, ri * T : ri * T + T, :].astype(F32) for i in range(NF)]
         for i, part in enumerate(butterfly(parts)):
-            at = (ri, pl.ds(i, T, stride=R), slice(None))
+            row = i % 4 * 2 + i // 4
+            at = (ri, pl.ds(row, T, stride=R), slice(None))
             out[at] = part + series_f[at]
     for c in own + second:
         c.wait_send()
@@ -449,9 +440,8 @@
             pltpu.VMEM((32, 128), F32),
             pltpu.VMEM((8, O), F32),
             pltpu.VMEM((128, G * O), BF16),
-            pltpu.VMEM((1152, 256), BF16),
-            pltpu.VMEM((NB + 2, 10 * C, 256), BF16),
-            pltpu.VMEM((NB, R * C, 256), BF16),
+            pltpu.VMEM((1024, 256), BF16),
+            pltpu.VMEM((N // 2 + 2, 10 * C, 128), BF16),
             pltpu.VMEM((NF, 2 * T, 128), BF16),
             pltpu.VMEM((NF, 2 * T, 128), BF16),
             pltpu.SemaphoreType.DMA((len(args),)),

time: 23.2 us -> 21.6 us (0.931)
  Pallas kernels: 22.4 us -> 20.7 us
    pallas_call x1, Pallas kernels: 22.4 us -> 20.7 us  [per_device(): pl.pallas_call(functools.partial(kernel, n_rows), out_shape=pltpu.VMEM((2...]
where the time goes in v6:
time: 21.6 us; the launch traced here: 21.4 us
  Pallas kernels  20.7 us (96%)
  other arithmetic  0.67 us (3%)
    pallas_call x1, Pallas kernels, per_device(): pl.pallas_call(functools.partial(kernel, n_rows), out_shape=pltpu.VMEM((2...  20.7 us
    concatenate x1, other arithmetic, per_device(): return jnp.concatenate((out[0], out[1]), axis=1).reshape(T, 1, R, 256)  0.67 us

profile of v6, /device:TPU:105, one launch (start us, length us, event | category | flops | bytes accessed | tf_op | source)
XLA Modules:
  0.0 21.4 jit_solution(3513906004729386462)
XLA Ops:
  0.0 20.7 %shard_map.100 = f32[2,128,128]{2,1,0:T(8,128)S(1)} custom-call(bf16[16,1,8,256]{3,2,1,0:T(8,128)(2,1)} %series.1, bf16[256,1024]{1,0:T(8,128)(2,1)} %constant.6.clone.fwd, bf16[256,256]{1,0:T(8,128)(2,1)} %constant.7.clone.inv, bf16[4,128,128]{2,1,0:T(8,128)(2,1)} %constant.8.clone.place, bf16[3,3,2,64]{3,2,1,0:T(2,128)(2,1)} %lift.1, f32[1,64]{1,0:T(1,128)} %bitcast.12, ...), custom_call_target="tpu_custom_call" | custom-call | tf_op jit(solution)/shard_map/pallas_call | solution.py:426
  20.8 0.7 %pad_maximum_fusion = f32[16,1,8,256]{3,2,1,0:T(8,128)} fusion(f32[16,1,8,128]{3,2,1,0:T(8,128)S(1)} %get-tuple-element.6, f32[16,1,8,128]{3,2,1,0:T(8,128)S(1)} %get-tuple-element.5), kind=kLoop, calls=%fused_computation | loop fusion | flops 32768 | bytes 262144 | tf_op jit(solution)/shard_map/concatenate | solution.py:459
  (1 shorter events, 0.0 us)

commit v7 on v6

--- a/solution.py
+++ b/solution.py
@@ -155,19 +155,6 @@
     has_below = r < n_rows - 1
     peers = [partner(f, m) for m in PARTNERS]
 
-    barrier = pltpu.get_barrier_semaphore()
-    for p in peers:
-        pl.semaphore_signal(barrier, inc=1, device_id={"frames": p}, device_id_type=MESH)
-
-    for has, near in ((has_above, above), (has_below, below)):
-
-        @pl.when(has)
-        def _():
-            for p in peers + [f]:
-                pl.semaphore_signal(
-                    barrier, inc=1, device_id={"frames": p, "rows": near}, device_id_type=MESH
-                )
-
     loads = [
         pltpu.make_async_copy(a, b, load_sem.at[i])
         for i, (a, b) in enumerate(
@@ -185,7 +172,22 @@
             )
         )
     ]
-    for c in loads:
+    loads[0].start()
+
+    barrier = pltpu.get_barrier_semaphore()
+    for p in peers:
+        pl.semaphore_signal(barrier, inc=1, device_id={"frames": p}, device_id_type=MESH)
+
+    for has, near in ((has_above, above), (has_below, below)):
+
+        @pl.when(has)
+        def _():
+            for p in peers + [f]:
+                pl.semaphore_signal(
+                    barrier, inc=1, device_id={"frames": p, "rows": near}, device_id_type=MESH
+                )
+
+    for c in loads[1:]:
         c.start()
 
     loads[0].wait()
@@ -230,7 +232,7 @@
         for side, near in ((0, below), (1, above))
     )
 
-    for c in own:
+    for c in own[:3]:
         c.start()
 
     @pl.when(has_below)
@@ -242,6 +244,9 @@
     def _():
         for c in up:
             c.start()
+
+    for c in own[3:]:
+        c.start()
 
     got[f] = sent[f]
 
@@ -305,6 +310,41 @@
 
     for c in own:
         c.wait_recv()
+    for ri in range(2):
+        xt[2 * C : 10 * C, ri * 128 : ri * 128 + 128] = (
+            got[:, ri * T : ri * T + T, :].reshape(NF * T, 128).T
+        )
+    inner = jnp.dot(xt[2 * C : 10 * C, :], fwd_v[...], preferred_element_type=F32).astype(BF16)
+    for g in range(NG):
+        spec[g, 2 * C : 10 * C, :] = inner[:, g * 128 : g * 128 + 128]
+
+    lane = lax.broadcasted_iota(jnp.int32, (10 * C, 128), 1)
+    top = jnp.full((C, 128), jnp.where(has_above, 1.0, 0.0), F32).astype(BF16)
+    bottom = jnp.full((C, 128), jnp.where(has_below, 1.0, 0.0), F32).astype(BF16)
+
+    def lift_rows(parts):
+        patch = []
+        for g in range(NG):
+            for lo, n, _ in parts:
+                rows = [spec[g, lo + b * C : lo + b * C + n, :] for b in range(3)]
+                at = lane[:n]
+                patch.append(
+                    jnp.where(at < 2 * W, rows[0], jnp.where(at < 4 * W, rows[1], rows[2]))
+                )
+        patch = jnp.concatenate(patch, axis=0)
+        for q in range(G // KB):
+            h = jnp.dot(patch, lift_m[:, q * 256 : q * 256 + 256], preferred_element_type=F32)
+            h = jnp.maximum(h + lift_bias4, 0.0).astype(BF16)
+            at = 0
+            for g in range(NG):
+                for lo, n, keep in parts:
+                    for half in range(2):
+                        kp = (g * KB + q) * 2 + half + 1
+                        piece = h[at : at + n, half * 128 : half * 128 + 128]
+                        hid[kp, lo : lo + n, :] = piece if keep is None else piece * keep
+                    at += n
+
+    lift_rows([(2 * C, 6 * C, None)])
 
     @pl.when(has_above)
     def _():
@@ -318,35 +358,18 @@
 
     quarter = lax.broadcasted_iota(jnp.int32, (NF * T, 128), 1) // (2 * C)
     near = jnp.where(quarter < 2, halo[1].reshape(NF * T, 128), halo[0].reshape(NF * T, 128)).T
-    for ri in range(2):
-        at = slice(ri * 128, ri * 128 + 128)
-        xt[: 2 * C, at] = near[(2 + ri) * 2 * C : (3 + ri) * 2 * C]
-        xt[2 * C : 10 * C, at] = got[:, ri * T : ri * T + T, :].reshape(NF * T, 128).T
-        xt[10 * C :, at] = near[ri * 2 * C : (1 + ri) * 2 * C]
-    spectrum = jnp.dot(xt[...], fwd_v[...], preferred_element_type=F32).astype(BF16)
+    ends_t = jnp.concatenate(
+        [
+            jnp.concatenate([near[(i + ri) * 2 * C : (i + ri + 1) * 2 * C] for ri in range(2)], axis=1)
+            for i in (2, 0)
+        ],
+        axis=0,
+    )
+    outer = jnp.dot(ends_t, fwd_v[...], preferred_element_type=F32).astype(BF16)
     for g in range(NG):
-        spec[g] = spectrum[:, g * 128 : g * 128 + 128]
-
-    lane = lax.broadcasted_iota(jnp.int32, (10 * C, 128), 1)
-
-    patch = []
-    for g in range(NG):
-        rows = [spec[g, b * C : b * C + 10 * C, :] for b in range(3)]
-        patch.append(jnp.where(lane < 2 * W, rows[0], jnp.where(lane < 4 * W, rows[1], rows[2])))
-    patch = jnp.concatenate(patch, axis=0)
-    top = jnp.full((C, 128), jnp.where(has_above, 1.0, 0.0), F32).astype(BF16)
-    bottom = jnp.full((C, 128), jnp.where(has_below, 1.0, 0.0), F32).astype(BF16)
-    for q in range(G // KB):
-        h = jnp.dot(patch, lift_m[:, q * 256 : q * 256 + 256], preferred_element_type=F32)
-        h = jnp.maximum(h + lift_bias4, 0.0).astype(BF16)
-        for g in range(NG):
-            at = g * 10 * C
-            for half in range(2):
-                kp = (g * KB + q) * 2 + half + 1
-                cols = slice(half * 128, half * 128 + 128)
-                hid[kp, :C, :] = h[at : at + C, cols] * top
-                hid[kp, C : 9 * C, :] = h[at + C : at + 9 * C, cols]
-                hid[kp, 9 * C :, :] = h[at + 9 * C : at + 10 * C, cols] * bottom
+        spec[g, : 2 * C, :] = outer[: 2 * C, g * 128 : g * 128 + 128]
+        spec[g, 10 * C :, :] = outer[2 * C :, g * 128 : g * 128 + 128]
+    lift_rows([(0, C, top), (C, C, None), (8 * C, C, None), (9 * C, C, bottom)])
 
     blocks = []
     for kp in range(1, N // 2 + 1):

time: 21.6 us -> 21.2 us (0.981)
  Pallas kernels: 20.7 us -> 20.3 us
    pallas_call x1, Pallas kernels: 20.7 us -> 20.3 us  [per_device(): pl.pallas_call(functools.partial(kernel, n_rows), out_shape=pltpu.VMEM((2...]
where the time goes in v7:
time: 21.2 us; the launch traced here: 21 us
  Pallas kernels  20.3 us (96%)
  other arithmetic  0.67 us (3%)
    pallas_call x1, Pallas kernels, per_device(): pl.pallas_call(functools.partial(kernel, n_rows), out_shape=pltpu.VMEM((2...  20.3 us
    concatenate x1, other arithmetic, per_device(): return jnp.concatenate((out[0], out[1]), axis=1).reshape(T, 1, R, 256)  0.67 us

profile of v7, /device:TPU:105, one launch (start us, length us, event | category | flops | bytes accessed | tf_op | source)
XLA Modules:
  0.0 21.0 jit_solution(15651301707160258736)
XLA Ops:
  0.0 20.3 %shard_map.100 = f32[2,128,128]{2,1,0:T(8,128)S(1)} custom-call(bf16[16,1,8,256]{3,2,1,0:T(8,128)(2,1)} %series.1, bf16[256,1024]{1,0:T(8,128)(2,1)} %constant.6.clone.fwd, bf16[256,256]{1,0:T(8,128)(2,1)} %constant.7.clone.inv, bf16[4,128,128]{2,1,0:T(8,128)(2,1)} %constant.8.clone.place, bf16[3,3,2,64]{3,2,1,0:T(2,128)(2,1)} %lift.1, f32[1,64]{1,0:T(1,128)} %bitcast.12, ...), custom_call_target="tpu_custom_call" | custom-call | tf_op jit(solution)/shard_map/pallas_call | solution.py:449
  20.3 0.7 %pad_maximum_fusion = f32[16,1,8,256]{3,2,1,0:T(8,128)} fusion(f32[16,1,8,128]{3,2,1,0:T(8,128)S(1)} %get-tuple-element.6, f32[16,1,8,128]{3,2,1,0:T(8,128)S(1)} %get-tuple-element.5), kind=kLoop, calls=%fused_computation | loop fusion | flops 32768 | bytes 262144 | tf_op jit(solution)/shard_map/concatenate | solution.py:482
  (1 shorter events, 0.0 us)

commit v8 on v7

--- a/solution.py
+++ b/solution.py
@@ -378,8 +378,12 @@
         for rp in range(R // 2):
             window = [slice((2 * rp + w) * C, (2 * rp + w + 1) * C) for w in range(4)]
             blocks.append(jnp.concatenate([x[at] for at in window for x in (here, beside)], axis=1))
-    mixed = jnp.dot(jnp.concatenate(blocks, axis=0), mix_m[...], preferred_element_type=F32)
-    mixed = jnp.maximum(mixed + mix_bias4, 0.0).astype(BF16)
+    half = len(blocks) // 2
+    mixed = []
+    for part in (blocks[:half], blocks[half:]):
+        total = jnp.dot(jnp.concatenate(part, axis=0), mix_m[...], preferred_element_type=F32)
+        mixed.append(jnp.maximum(total + mix_bias4, 0.0).astype(BF16))
+    mixed = jnp.concatenate(mixed, axis=0)
     u = lax.dot_general(
         proj4, mixed, (((1,), (1,)), ((), ())), preferred_element_type=F32
     )

time: 21.2 us -> 21.2 us (level)
  no operation moved by 1% of the time
where the time goes in v8:
time: 21.2 us; the launch traced here: 20.9 us
  Pallas kernels  20.2 us (95%)
  other arithmetic  0.67 us (3%)
    pallas_call x1, Pallas kernels, per_device(): pl.pallas_call(functools.partial(kernel, n_rows), out_shape=pltpu.VMEM((2...  20.2 us
    concatenate x1, other arithmetic, per_device(): return jnp.concatenate((out[0], out[1]), axis=1).reshape(T, 1, R, 256)  0.67 us

profile of v8, /device:TPU:105, one launch (start us, length us, event | category | flops | bytes accessed | tf_op | source)
XLA Modules:
  0.0 20.9 jit_solution(1076366776708511592)
XLA Ops:
  0.0 20.2 %shard_map.100 = f32[2,128,128]{2,1,0:T(8,128)S(1)} custom-call(bf16[16,1,8,256]{3,2,1,0:T(8,128)(2,1)} %series.1, bf16[256,1024]{1,0:T(8,128)(2,1)} %constant.6.clone.fwd, bf16[256,256]{1,0:T(8,128)(2,1)} %constant.7.clone.inv, bf16[4,128,128]{2,1,0:T(8,128)(2,1)} %constant.8.clone.place, bf16[3,3,2,64]{3,2,1,0:T(2,128)(2,1)} %lift.1, f32[1,64]{1,0:T(1,128)} %bitcast.12, ...), custom_call_target="tpu_custom_call" | custom-call | tf_op jit(solution)/shard_map/pallas_call | solution.py:453
  20.2 0.7 %pad_maximum_fusion = f32[16,1,8,256]{3,2,1,0:T(8,128)} fusion(f32[16,1,8,128]{3,2,1,0:T(8,128)S(1)} %get-tuple-element.6, f32[16,1,8,128]{3,2,1,0:T(8,128)S(1)} %get-tuple-element.5), kind=kLoop, calls=%fused_computation | loop fusion | flops 32768 | bytes 262144 | tf_op jit(solution)/shard_map/concatenate | solution.py:486
  (1 shorter events, 0.0 us)

commit v9 on v8

--- a/solution.py
+++ b/solution.py
@@ -378,9 +378,9 @@
         for rp in range(R // 2):
             window = [slice((2 * rp + w) * C, (2 * rp + w + 1) * C) for w in range(4)]
             blocks.append(jnp.concatenate([x[at] for at in window for x in (here, beside)], axis=1))
-    half = len(blocks) // 2
+    size = len(blocks) // 4
     mixed = []
-    for part in (blocks[:half], blocks[half:]):
+    for part in (blocks[i * size : (i + 1) * size] for i in range(4)):
         total = jnp.dot(jnp.concatenate(part, axis=0), mix_m[...], preferred_element_type=F32)
         mixed.append(jnp.maximum(total + mix_bias4, 0.0).astype(BF16))
     mixed = jnp.concatenate(mixed, axis=0)

time: 21.2 us -> 21.1 us (level)
  no operation moved by 1% of the time
where the time goes in v9:
time: 21.1 us; the launch traced here: 20.8 us
  Pallas kernels  20.1 us (95%)
  other arithmetic  0.67 us (3%)
    pallas_call x1, Pallas kernels, per_device(): pl.pallas_call(functools.partial(kernel, n_rows), out_shape=pltpu.VMEM((2...  20.1 us
    concatenate x1, other arithmetic, per_device(): return jnp.concatenate((out[0], out[1]), axis=1).reshape(T, 1, R, 256)  0.67 us

profile of v9, /device:TPU:105, one launch (start us, length us, event | category | flops | bytes accessed | tf_op | source)
XLA Modules:
  0.0 20.8 jit_solution(7130770190566247336)
XLA Ops:
  0.0 20.1 %shard_map.100 = f32[2,128,128]{2,1,0:T(8,128)S(1)} custom-call(bf16[16,1,8,256]{3,2,1,0:T(8,128)(2,1)} %series.1, bf16[256,1024]{1,0:T(8,128)(2,1)} %constant.6.clone.fwd, bf16[256,256]{1,0:T(8,128)(2,1)} %constant.7.clone.inv, bf16[4,128,128]{2,1,0:T(8,128)(2,1)} %constant.8.clone.place, bf16[3,3,2,64]{3,2,1,0:T(2,128)(2,1)} %lift.1, f32[1,64]{1,0:T(1,128)} %bitcast.12, ...), custom_call_target="tpu_custom_call" | custom-call | tf_op jit(solution)/shard_map/pallas_call | solution.py:453
  20.2 0.7 %pad_maximum_fusion = f32[16,1,8,256]{3,2,1,0:T(8,128)} fusion(f32[16,1,8,128]{3,2,1,0:T(8,128)S(1)} %get-tuple-element.6, f32[16,1,8,128]{3,2,1,0:T(8,128)S(1)} %get-tuple-element.5), kind=kLoop, calls=%fused_computation | loop fusion | flops 32768 | bytes 262144 | tf_op jit(solution)/shard_map/concatenate | solution.py:486
  (1 shorter events, 0.0 us)

commit v10 on v9

--- a/solution.py
+++ b/solution.py
@@ -378,9 +378,9 @@
         for rp in range(R // 2):
             window = [slice((2 * rp + w) * C, (2 * rp + w + 1) * C) for w in range(4)]
             blocks.append(jnp.concatenate([x[at] for at in window for x in (here, beside)], axis=1))
-    size = len(blocks) // 4
+    size = len(blocks) // 8
     mixed = []
-    for part in (blocks[i * size : (i + 1) * size] for i in range(4)):
+    for part in (blocks[i * size : (i + 1) * size] for i in range(8)):
         total = jnp.dot(jnp.concatenate(part, axis=0), mix_m[...], preferred_element_type=F32)
         mixed.append(jnp.maximum(total + mix_bias4, 0.0).astype(BF16))
     mixed = jnp.concatenate(mixed, axis=0)

time: 21.1 us -> 21.1 us (level)
  no operation moved by 1% of the time
where the time goes in v10:
time: 21.1 us; the launch traced here: 20.8 us
  Pallas kernels  20.1 us (95%)
  other arithmetic  0.67 us (3%)
    pallas_call x1, Pallas kernels, per_device(): pl.pallas_call(functools.partial(kernel, n_rows), out_shape=pltpu.VMEM((2...  20.1 us
    concatenate x1, other arithmetic, per_device(): return jnp.concatenate((out[0], out[1]), axis=1).reshape(T, 1, R, 256)  0.67 us

profile of v10, /device:TPU:105, one launch (start us, length us, event | category | flops | bytes accessed | tf_op | source)
XLA Modules:
  0.0 20.8 jit_solution(4119145037395792411)
XLA Ops:
  0.0 20.1 %shard_map.100 = f32[2,128,128]{2,1,0:T(8,128)S(1)} custom-call(bf16[16,1,8,256]{3,2,1,0:T(8,128)(2,1)} %series.1, bf16[256,1024]{1,0:T(8,128)(2,1)} %constant.6.clone.fwd, bf16[256,256]{1,0:T(8,128)(2,1)} %constant.7.clone.inv, bf16[4,128,128]{2,1,0:T(8,128)(2,1)} %constant.8.clone.place, bf16[3,3,2,64]{3,2,1,0:T(2,128)(2,1)} %lift.1, f32[1,64]{1,0:T(1,128)} %bitcast.12, ...), custom_call_target="tpu_custom_call" | custom-call | tf_op jit(solution)/shard_map/pallas_call | solution.py:453
  20.1 0.7 %pad_maximum_fusion = f32[16,1,8,256]{3,2,1,0:T(8,128)} fusion(f32[16,1,8,128]{3,2,1,0:T(8,128)S(1)} %get-tuple-element.6, f32[16,1,8,128]{3,2,1,0:T(8,128)S(1)} %get-tuple-element.5), kind=kLoop, calls=%fused_computation | loop fusion | flops 32768 | bytes 262144 | tf_op jit(solution)/shard_map/concatenate | solution.py:486
  (1 shorter events, 0.0 us)
